TPU v7x, 768 devices: a whole 4x8x12 slice. The times are simulated.
768 devices in a mesh: tile: 96 (over z, y), spec: 8 (over x, core).
Axes of the slice: x: 4, y: 8, z: 12, core: 2. Of those that a mesh axis runs over, the one named last changes fastest.
Arguments:
- spectra: float32 [864, 768, 128], P('spec', 'tile'), may hold values from 0.05 to 2
- wind_speed: float32 [768, 128], P('tile'), may hold values from 3 to 20
- wind_dir: float32 [768, 128], P('tile'), may hold values from -3.140625 to 3.140625
- sea_mask: int32 [768, 128], P('tile'), may hold values 0 or 1
- neighbours: int32 [768, 4], P('tile'), may hold values from -1 to 767, as said below
Outputs:
- spectra_next: float32 [864, 768, 128], P('spec', 'tile')
Inputs may be any that keep to these rules, and one draw needn't show every extreme that they name: Tiles come in aligned blocks of 8; block b is one row of the basin's tiles in shuffled order. A tile's north neighbour lies in block b - 1, its south neighbour in block b + 1, its west and east neighbours in block b; the relations are mutual (my north's south is me, my west's east is me). Block 0 has no north neighbours, the last block no south ones, one tile of each block no west neighbour and one no east neighbour.
All inputs are finite; a program needn't handle non-finite values. No bound on the sum of `sea_mask` on one device may be relied on, other than what follows from the above.
Results may differ from a plain program's by a relative error of at most 0.0003.
Values sent between devices are 32-bit elements; how exact they have to be, the bound alone decides.
A program may use at most 32 MiB of HBM per device.

v0:
```python
import math

import jax
import jax.numpy as jnp
from jax import lax
from jax.sharding import PartitionSpec as P

NDIR = 36
ROWS = 4
COLS = 32
SUBSTEPS = 4
SOURCE_ITERS = 3
COMPONENTS = 864


def padded(cells, sides, width):
    for axis, dim in sides:
        count = lax.axis_size(axis)
        ends = count - 1
        head = lax.slice_in_dim(cells, 0, width, axis=dim)
        tail = lax.slice_in_dim(cells, cells.shape[dim] - width, cells.shape[dim], axis=dim)
        cells = jnp.concatenate(
            [
                lax.ppermute(tail, axis, [(i, (i + 1) % count) for i in range(ends)]),
                cells,
                lax.ppermute(head, axis, [((i + 1) % count, i) for i in range(ends)]),
            ],
            axis=dim,
        )
    return cells


def comp_tables(first, count):
    index = first + jnp.arange(count, dtype=jnp.int32)
    freq_index = (index // NDIR).astype(jnp.float32)
    direction = ((index % NDIR).astype(jnp.float32) + 0.5) * (2.0 * math.pi / NDIR)
    ratio = jnp.power(jnp.float32(1.1), freq_index)
    speed = 0.65 / ratio
    return (ratio, direction, speed * jnp.cos(direction), speed * jnp.sin(direction))


def advect(energy, north_rim, south_rim, west_col, east_col, east_speed, south_speed, sea):
    above = jnp.concatenate([north_rim[:, :, None, :], energy[:, :, :-1, :]], axis=2)
    beneath = jnp.concatenate([energy[:, :, 1:, :], south_rim[:, :, None, :]], axis=2)
    leftward = jnp.concatenate([west_col[:, :, :, None], energy[:, :, :, :-1]], axis=3)
    rightward = jnp.concatenate([energy[:, :, :, 1:], east_col[:, :, :, None]], axis=3)
    upwind_x = jnp.where(east_speed > 0, leftward, rightward)
    upwind_y = jnp.where(south_speed > 0, above, beneath)
    moved = (
        energy
        - jnp.abs(east_speed) * (energy - upwind_x)
        - jnp.abs(south_speed) * (energy - upwind_y)
    )
    return moved * sea[None]


def moment_terms(energy, ratio):
    return (jnp.sum(ratio * energy, axis=0), jnp.sum(ratio * ratio * energy, axis=0))


def source_step(energy, total, weighted, ratio, direction, speed_w, dir_w, sea):
    first_moment = total / COMPONENTS
    second_moment = weighted / COMPONENTS
    mean_ratio = (second_moment + 0.1) / (first_moment + 0.1)
    cosine = jnp.cos(direction - dir_w[None])
    grow = 0.03 * speed_w[None] * jnp.maximum(cosine, 0.0) * jnp.sqrt(ratio)
    damp = 0.25 * first_moment[None] * jnp.square(ratio / mean_ratio[None])
    change = 0.2 * (grow - damp) * energy
    limit = 0.08 / ratio
    change = jnp.clip(change, -limit, limit)
    return jnp.maximum(energy + change, 0.0) * sea[None]


def pick(rows, local_index, ids):
    valid = (ids >= 0).astype(jnp.float32)
    safe_index = jnp.clip(local_index, 0, rows.shape[1] - 1)
    return jnp.take(rows, safe_index, axis=1) * valid[None, :, None]


def body(spectra, wind_speed, wind_dir, sea_mask, neighbours):
    comp_dev, tiles_dev, points = spectra.shape
    spec_index = lax.axis_index("spec")
    block_index = lax.axis_index("tile")
    ratio, direction, east_speed, south_speed = comp_tables(spec_index * comp_dev, comp_dev)
    east_speed = east_speed[:, None, None, None]
    south_speed = south_speed[:, None, None, None]
    sea_flat = sea_mask.astype(jnp.float32)
    sea = sea_flat.reshape(tiles_dev, ROWS, COLS)
    energy = spectra.reshape(comp_dev, tiles_dev, ROWS, COLS) * sea[None]
    base = block_index * tiles_dev
    north_ids = neighbours[:, 0]
    south_ids = neighbours[:, 1]
    west_ids = neighbours[:, 2]
    east_ids = neighbours[:, 3]
    for step in range(SUBSTEPS):
        bottom = energy[:, :, ROWS - 1, :]
        top_row = energy[:, :, 0, :]
        paired = jnp.concatenate([bottom, top_row], axis=2)
        widened = padded(paired, (("tile", 1),), tiles_dev)
        north_rim = pick(widened[:, :, :COLS], north_ids - (base - tiles_dev), north_ids)
        south_rim = pick(widened[:, :, COLS:], south_ids - (base - tiles_dev), south_ids)
        west_col = pick(energy[:, :, :, COLS - 1], west_ids - base, west_ids)
        east_col = pick(energy[:, :, :, 0], east_ids - base, east_ids)
        energy = advect(
            energy, north_rim, south_rim, west_col, east_col, east_speed, south_speed, sea
        )
    flat = energy.reshape(comp_dev, tiles_dev, points)
    gathered = lax.all_to_all(flat, "spec", split_axis=1, concat_axis=0, tiled=True)
    share = gathered.shape[1]
    start = spec_index * share
    speed_part = lax.dynamic_slice_in_dim(wind_speed, start, share, 0)
    dir_part = lax.dynamic_slice_in_dim(wind_dir, start, share, 0)
    sea_part = lax.dynamic_slice_in_dim(sea_flat, start, share, 0)
    all_ratio, all_direction, unused_east, unused_south = comp_tables(0, gathered.shape[0])
    all_ratio = all_ratio[:, None, None]
    all_direction = all_direction[:, None, None]
    for step in range(SOURCE_ITERS):
        total, weighted = moment_terms(gathered, all_ratio)
        gathered = source_step(
            gathered, total, weighted, all_ratio, all_direction, speed_part, dir_part, sea_part
        )
    result = lax.all_to_all(gathered, "spec", split_axis=0, concat_axis=1, tiled=True)
    return result


def solution(mesh):
    placed = (
        P("spec", "tile", None),
        P("tile", None),
        P("tile", None),
        P("tile", None),
        P("tile", None),
    )
    return jax.shard_map(
        body, mesh=mesh, in_specs=placed, out_specs=P("spec", "tile", None), check_vma=False
    )
```

profile of v0, /device:TPU:256, one launch (start us, length us, event | category | flops | bytes accessed | tf_op | source)
XLA Modules:
  0.0 151.1 jit_solution(18093559047862438737)
XLA Ops:
  1.3 1.2 copy.62
  2.8 3.5 %collective-permute-start = (f32[108,8,64]{0,2,1:T(8,128)S(1)}, f32[108,8,64]{0,2,1:T(8,128)S(1)}, u32[]{:S(2)}, u32[]{:S(2)}) collective-permute-start(f32[108,8,64]{0,2,1:T(8,128)S(1)} %pad_maximum_fusion.20), channel_id=1, source_target_pairs={{0,8},{8,16},{16,24},{24,32},{32,40},{40,48},{48,56},{56,64},{64,7... | collective-permute-start | bytes 663560 | tf_op jit(solution)/shard_map/ppermute | solution.py:24
  6.3 5.7 %collective-permute-start.1 = (f32[108,8,64]{0,2,1:T(8,128)S(1)}, f32[108,8,64]{0,2,1:T(8,128)S(1)}, u32[]{:S(2)}, u32[]{:S(2)}) collective-permute-start(f32[108,8,64]{0,2,1:T(8,128)S(1)} %pad_maximum_fusion.20), channel_id=1, source_target_pairs={{8,0},{16,8},{24,16},{32,24},{40,32},{48,40},{56,48},{64,56},{72,6... | collective-permute-start | bytes 663560 | tf_op jit(solution)/shard_map/ppermute | solution.py:26
  18.3 1.3 fusion.81
  22.8 2.5 %subtract_multiply_fusion.2 = (f32[108,8,4,32]{0,3,1,2:T(8,128)S(1)}, f32[108,8,4,32]{0,3,1,2:T(8,128)S(1)}, f32[108,8,4,32]{0,3,1,2:T(8,128)S(1)}, f32[108,8,4,32]{0,3,1,2:T(8,128)}, f32[108,8,4,32]{0,3,1,2:T(8,128)S(1)}) fusion(f32[108]{0:T(128)S(1)} %copy-done.71, f32[108]{0:T(128)S(1)} %copy-done.67, f32[8,4,32]{2,0,1:T(8,128)S(1)} %copy.64, ...), kind=kLoop, calls=%fused_computation.75 | loop fusion | flops 1548288 | bytes 4428856 | tf_op jit(solution)/shard_map/mul | solution.py:54
  26.0 1.9 %collective-permute-start.2 = (f32[108,8,64]{0,2,1:T(8,128)}, f32[108,8,64]{0,2,1:T(8,128)}, u32[]{:S(2)}, u32[]{:S(2)}) collective-permute-start(f32[108,8,64]{0,2,1:T(8,128)} %pad_maximum_fusion.21), channel_id=1, source_target_pairs={{0,8},{8,16},{16,24},{24,32},{32,40},{40,48},{48,56},{56,64},{64,7... | collective-permute-start | bytes 663560 | tf_op jit(solution)/shard_map/ppermute | solution.py:24
  28.0 7.2 %collective-permute-start.3 = (f32[108,8,64]{0,2,1:T(8,128)}, f32[108,8,64]{0,2,1:T(8,128)}, u32[]{:S(2)}, u32[]{:S(2)}) collective-permute-start(f32[108,8,64]{0,2,1:T(8,128)} %pad_maximum_fusion.21), channel_id=1, source_target_pairs={{8,0},{16,8},{24,16},{32,24},{40,32},{48,40},{56,48},{64,56},{72,6... | collective-permute-start | bytes 663560 | tf_op jit(solution)/shard_map/ppermute | solution.py:26
  35.2 1.1 fusion.105
  42.1 1.1 pad_maximum_fusion.1
  44.0 1.4 fusion.54
  47.8 3.1 %subtract_multiply_fusion.1 = (f32[108,8,4,32]{0,3,1,2:T(8,128)S(1)}, f32[108,8,4,32]{0,3,1,2:T(8,128)}, f32[108,8,4,32]{0,3,1,2:T(8,128)}, f32[108,8,4,32]{0,3,1,2:T(8,128)}, f32[108,8,4,32]{0,3,1,2:T(8,128)}) fusion(f32[108,8,4,32]{0,3,1,2:T(8,128)S(1)} %get-tuple-element.21, f32[108]{0:T(128)S(1)} %copy-done.72, f32[108]{0:T(128)S(1)} %copy-done.68, ...), kind=kLoop, calls=%fused_computation.74 | loop fusion | flops 1437696 | bytes 4428856 | tf_op jit(solution)/shard_map/mul | solution.py:54
  51.6 1.9 %collective-permute-start.4 = (f32[108,8,64]{0,2,1:T(8,128)}, f32[108,8,64]{0,2,1:T(8,128)}, u32[]{:S(2)}, u32[]{:S(2)}) collective-permute-start(f32[108,8,64]{0,2,1:T(8,128)} %pad_maximum_fusion.22), channel_id=1, source_target_pairs={{0,8},{8,16},{16,24},{24,32},{32,40},{40,48},{48,56},{56,64},{64,7... | collective-permute-start | bytes 663560 | tf_op jit(solution)/shard_map/ppermute | solution.py:24
  53.6 7.2 %collective-permute-start.5 = (f32[108,8,64]{0,2,1:T(8,128)}, f32[108,8,64]{0,2,1:T(8,128)}, u32[]{:S(2)}, u32[]{:S(2)}) collective-permute-start(f32[108,8,64]{0,2,1:T(8,128)} %pad_maximum_fusion.22), channel_id=1, source_target_pairs={{8,0},{16,8},{24,16},{32,24},{40,32},{48,40},{56,48},{64,56},{72,6... | collective-permute-start | bytes 663560 | tf_op jit(solution)/shard_map/ppermute | solution.py:26
  70.3 1.1 pad_maximum_fusion.2
  72.1 1.4 fusion.52
  75.9 3.1 %subtract_multiply_fusion = (f32[108,8,4,32]{0,3,1,2:T(8,128)S(1)}, f32[108,8,4,32]{0,3,1,2:T(8,128)}, f32[108,8,4,32]{0,3,1,2:T(8,128)}, f32[108,8,4,32]{0,3,1,2:T(8,128)}, f32[108,8,4,32]{0,3,1,2:T(8,128)}) fusion(f32[108,8,4,32]{0,3,1,2:T(8,128)S(1)} %get-tuple-element.18, f32[108]{0:T(128)S(1)} %copy-done.73, f32[108]{0:T(128)S(1)} %copy-done.69, ...), kind=kLoop, calls=%fused_computation.73 | loop fusion | flops 1437696 | bytes 4428856 | tf_op jit(solution)/shard_map/mul | solution.py:54
  80.9 1.9 %collective-permute-start.6 = (f32[108,8,64]{0,2,1:T(8,128)}, f32[108,8,64]{0,2,1:T(8,128)}, u32[]{:S(2)}, u32[]{:S(2)}) collective-permute-start(f32[108,8,64]{0,2,1:T(8,128)} %pad_maximum_fusion.23), channel_id=1, source_target_pairs={{0,8},{8,16},{16,24},{24,32},{32,40},{40,48},{48,56},{56,64},{64,7... | collective-permute-start | bytes 663560 | tf_op jit(solution)/shard_map/ppermute | solution.py:24
  82.9 7.2 %collective-permute-start.7 = (f32[108,8,64]{0,2,1:T(8,128)}, f32[108,8,64]{0,2,1:T(8,128)}, u32[]{:S(2)}, u32[]{:S(2)}) collective-permute-start(f32[108,8,64]{0,2,1:T(8,128)} %pad_maximum_fusion.23), channel_id=1, source_target_pairs={{8,0},{16,8},{24,16},{32,24},{40,32},{48,40},{56,48},{64,56},{72,6... | collective-permute-start | bytes 663560 | tf_op jit(solution)/shard_map/ppermute | solution.py:26
  91.0 1.1 pad_maximum_fusion.16
  93.8 1.1 pad_maximum_fusion.17
  101.7 1.1 pad_maximum_fusion.3
  105.5 1.8 %gather_fusion.15 = f32[8,108,32]{1,2,0:T(8,128)S(1)} fusion(f32[108,24,32]{0,2,1:T(8,128)} %get-tuple-element.33, s32[1024]{0:T(1024)} %copy-done.55), kind=kCustom, calls=%fused_computation.15.clone | custom fusion | bytes 221216 | tf_op jit(solution)/shard_map/jit(_take)/gather | solution.py:77
  107.4 1.1 pad_maximum_fusion.19
  109.8 3.4 %fusion.3 = f32[108,8,128]{0,2,1:T(8,128)} fusion(f32[108,8,4,32]{0,3,2,1:T(8,128)S(1)} %copy.98, f32[108,8,4,32]{0,3,2,1:T(8,128)} %copy.97, f32[108,8,4,32]{0,3,2,1:T(8,128)} %copy.96, f32[108,8,4,32]{0,3,2,1:T(8,128)S(1)} %copy-done.5, f32[108,8,4,32]{0,3,2,1:T(8,128)} %copy.89, f32[108,8,4,32]{0,3,2,1:T(8,128)} %copy.88, f32[108,8,4,32]{0,3,2,1:T(8,128)} %copy.87, ...), kind=kLoop, calls=%fused_computation.40 | loop fusion | flops 4091904 | bytes 7967800 | tf_op jit(solution)/shard_map/mul | solution.py:54
  113.2 2.0 %copy.99 = f32[108,8,128]{2,0,1:T(8,128)} copy(f32[108,8,128]{0,2,1:T(8,128)} %fusion.3) | data formatting | bytes 884736 | tf_op jit(solution)/shard_map/mul | solution.py:54
  115.2 4.3 %all-to-all-start = ((f32[108,8,128]{2,0,1:T(8,128)}), f32[108,8,128]{2,0,1:T(8,128)S(1)}, u32[]{:S(2)}, u32[]{:S(2)}) async-start(f32[108,8,128]{2,0,1:T(8,128)} %copy.99), calls=%async_computation | async-start | bytes 917504 | tf_op jit(solution)/shard_map/all_to_all | solution.py:108
  119.6 9.6 %all-to-all-done = f32[108,8,128]{2,0,1:T(8,128)S(1)} async-done(((f32[108,8,128]{2,0,1:T(8,128)}), f32[108,8,128]{2,0,1:T(8,128)S(1)}, u32[]{:S(2)}, u32[]{:S(2)}) %all-to-all-start) | async-done | bytes 442400 | tf_op jit(solution)/shard_map/all_to_all | solution.py:108
  130.2 1.9 %multiply_reduce_fusion.2 = (f32[128]{0:T(128)S(1)}, f32[128]{0:T(128)S(1)}, f32[864,1,128]{2,0,1:T(8,128)S(1)}) fusion(f32[864]{0:T(1024)S(1)} %get-tuple-element.105, f32[864]{0:T(1024)S(1)} %get-tuple-element.104, f32[128]{0:T(128)S(1)} %fusion.83, f32[864,1,128]{2,0,1:T(8,128)S(1)} %all_to_all.29, f32[128]{0:T(128)S(1)} %get-tuple-element.93, ...), kind=kLoop, calls=%fused_computation.104 | loop fusion | flops 2100992 | bytes 909056 | tf_op jit(solution)/shard_map/reduce_sum | solution.py:58
  132.2 2.0 %multiply_reduce_fusion = (f32[128]{0:T(128)S(1)}, f32[128]{0:T(128)S(1)}, f32[864,1,128]{2,0,1:T(8,128)S(1)}) fusion(f32[864]{0:T(1024)S(1)} %get-tuple-element.105, f32[864]{0:T(1024)S(1)} %get-tuple-element.104, f32[128]{0:T(128)S(1)} %fusion.83, f32[864,1,128]{2,0,1:T(8,128)S(1)} %get-tuple-element.14, f32[128]{0:T(128)S(1)} %get-tuple-element.91, ...), kind=kLoop, calls=%fused_computation.101 | loop fusion | flops 2100992 | bytes 909056 | tf_op jit(solution)/shard_map/reduce_sum | solution.py:58
  134.1 1.9 %maximum_multiply_fusion = f32[864,1,128]{2,0,1:T(8,128)S(1)} fusion(f32[864,1,128]{2,0,1:T(8,128)S(1)} %get-tuple-element.13, f32[128]{0:T(128)S(1)} %get-tuple-element.89, f32[128]{0:T(128)S(1)} %get-tuple-element.88, f32[128]{0:T(128)S(1)} %fusion.83, f32[864]{0:T(1024)S(1)} %get-tuple-element.104, f32[864]{0:T(1024)S(1)} %get-tuple-element.108, ...), kind=kLoop, calls=%fused_computation.100 | loop fusion | flops 1658880 | bytes 904576 | tf_op jit(solution)/shard_map/mul | solution.py:71
  136.0 11.9 %all_to_all.36 = f32[864,1,128]{2,1,0:T(1,128)S(1)} all-to-all(f32[864,1,128]{2,1,0:T(1,128)S(1)} %bitcast.263), channel_id=1, replica_groups=mesh['tile'=96,'spec'=8] {'spec'}, dimensions={0} | all-to-all | bytes 884736 | tf_op jit(solution)/shard_map/all_to_all | solution.py:122
  148.4 1.7 %reduce.9 = f32[864,128]{1,0:T(8,128)S(1)} reduce(f32[864,1,128]{2,1,0:T(1,128)S(1)} %all_to_all.36, f32[]{:T(128)} %broadcast.2081), dimensions={1}, to_apply=%all_to_all.30.reduce_sub_computation.3 | reduce | bytes 884740 | tf_op jit(solution)/shard_map/all_to_all | solution.py:122
  (272 shorter events, 50.9 us)
Async XLA Ops:
  2.8 17.7 %collective-permute-start = (f32[108,8,64]{0,2,1:T(8,128)S(1)}, f32[108,8,64]{0,2,1:T(8,128)S(1)}, u32[]{:S(2)}, u32[]{:S(2)}) collective-permute-start(f32[108,8,64]{0,2,1:T(8,128)S(1)} %pad_maximum_fusion.20), channel_id=1, source_target_pairs={{0,8},{8,16},{16,24},{24,32},{32,40},{40,48},{48,56},{56,64},{64,7... | collective-permute-start | bytes 663560 | tf_op jit(solution)/shard_map/ppermute | solution.py:24
  6.3 14.2 %collective-permute-start.1 = (f32[108,8,64]{0,2,1:T(8,128)S(1)}, f32[108,8,64]{0,2,1:T(8,128)S(1)}, u32[]{:S(2)}, u32[]{:S(2)}) collective-permute-start(f32[108,8,64]{0,2,1:T(8,128)S(1)} %pad_maximum_fusion.20), channel_id=1, source_target_pairs={{8,0},{16,8},{24,16},{32,24},{40,32},{48,40},{56,48},{64,56},{72,6... | collective-permute-start | bytes 663560 | tf_op jit(solution)/shard_map/ppermute | solution.py:26
  15.0 1.9 %copy-start.39 = (f32[8]{0:T(128)}, f32[8]{0:T(128)S(1)}, u32[]{:S(2)}) copy-start(f32[8]{0:T(128)S(1)} %get-tuple-element.79) | copy-start | bytes 100
  15.0 1.9 %copy-start.43 = (f32[8]{0:T(128)}, f32[8]{0:T(128)S(1)}, u32[]{:S(2)}) copy-start(f32[8]{0:T(128)S(1)} %get-tuple-element.78) | copy-start | bytes 100
  15.0 6.7 %copy-start.51 = (f32[8]{0:T(128)}, f32[8]{0:T(128)S(1)}, u32[]{:S(2)}) copy-start(f32[8]{0:T(128)S(1)} %get-tuple-element.81) | copy-start | bytes 100
  15.0 6.7 %copy-start.53 = (f32[8]{0:T(128)}, f32[8]{0:T(128)S(1)}, u32[]{:S(2)}) copy-start(f32[8]{0:T(128)S(1)} %get-tuple-element.80) | copy-start | bytes 100
  15.1 1.9 %copy-start.31 = (pred[8]{0:T(512)(128)(4,1)}, pred[8]{0:T(512)(128)(4,1)S(1)}, u32[]{:S(2)}) copy-start(pred[8]{0:T(512)(128)(4,1)S(1)} %get-tuple-element.86) | copy-start | bytes 28
  15.1 1.9 %copy-start.35 = (pred[8]{0:T(512)(128)(4,1)}, pred[8]{0:T(512)(128)(4,1)S(1)}, u32[]{:S(2)}) copy-start(pred[8]{0:T(512)(128)(4,1)S(1)} %get-tuple-element.30) | copy-start | bytes 28
  15.1 6.7 %copy-start.47 = (pred[8]{0:T(512)(128)(4,1)}, pred[8]{0:T(512)(128)(4,1)S(1)}, u32[]{:S(2)}) copy-start(pred[8]{0:T(512)(128)(4,1)S(1)} %get-tuple-element.82) | copy-start | bytes 28
  15.1 6.7 %copy-start.49 = (pred[8]{0:T(512)(128)(4,1)}, pred[8]{0:T(512)(128)(4,1)S(1)}, u32[]{:S(2)}) copy-start(pred[8]{0:T(512)(128)(4,1)S(1)} %get-tuple-element.84) | copy-start | bytes 28
  15.1 5.4 %copy-start.56 = (s32[1024]{0:T(1024)}, s32[1024]{0:T(1024)S(1)}, u32[]{:S(2)}) copy-start(s32[1024]{0:T(1024)S(1)} %pad_clamp_fusion.1) | copy-start | bytes 12292
  15.1 6.0 %copy-start.55 = (s32[1024]{0:T(1024)}, s32[1024]{0:T(1024)S(1)}, u32[]{:S(2)}) copy-start(s32[1024]{0:T(1024)S(1)} %pad_clamp_fusion) | copy-start | bytes 12292
  26.0 16.1 %collective-permute-start.2 = (f32[108,8,64]{0,2,1:T(8,128)}, f32[108,8,64]{0,2,1:T(8,128)}, u32[]{:S(2)}, u32[]{:S(2)}) collective-permute-start(f32[108,8,64]{0,2,1:T(8,128)} %pad_maximum_fusion.21), channel_id=1, source_target_pairs={{0,8},{8,16},{16,24},{24,32},{32,40},{40,48},{48,56},{56,64},{64,7... | collective-permute-start | bytes 663560 | tf_op jit(solution)/shard_map/ppermute | solution.py:24
  28.0 14.2 %collective-permute-start.3 = (f32[108,8,64]{0,2,1:T(8,128)}, f32[108,8,64]{0,2,1:T(8,128)}, u32[]{:S(2)}, u32[]{:S(2)}) collective-permute-start(f32[108,8,64]{0,2,1:T(8,128)} %pad_maximum_fusion.21), channel_id=1, source_target_pairs={{8,0},{16,8},{24,16},{32,24},{40,32},{48,40},{56,48},{64,56},{72,6... | collective-permute-start | bytes 663560 | tf_op jit(solution)/shard_map/ppermute | solution.py:26
  45.4 1.7 %copy-start.17 = (f32[108,8,3,32]{0,3,1,2:T(8,128)S(1)}, f32[108,8,3,32]{0,3,1,2:T(8,128)}, u32[]{:S(2)}) copy-start(f32[108,8,3,32]{0,3,1,2:T(8,128)} %get-tuple-element.66) | copy-start | bytes 995332
  51.6 18.6 %collective-permute-start.4 = (f32[108,8,64]{0,2,1:T(8,128)}, f32[108,8,64]{0,2,1:T(8,128)}, u32[]{:S(2)}, u32[]{:S(2)}) collective-permute-start(f32[108,8,64]{0,2,1:T(8,128)} %pad_maximum_fusion.22), channel_id=1, source_target_pairs={{0,8},{8,16},{16,24},{24,32},{32,40},{40,48},{48,56},{56,64},{64,7... | collective-permute-start | bytes 663560 | tf_op jit(solution)/shard_map/ppermute | solution.py:24
  53.6 16.7 %collective-permute-start.5 = (f32[108,8,64]{0,2,1:T(8,128)}, f32[108,8,64]{0,2,1:T(8,128)}, u32[]{:S(2)}, u32[]{:S(2)}) collective-permute-start(f32[108,8,64]{0,2,1:T(8,128)} %pad_maximum_fusion.22), channel_id=1, source_target_pairs={{8,0},{16,8},{24,16},{32,24},{40,32},{48,40},{56,48},{64,56},{72,6... | collective-permute-start | bytes 663560 | tf_op jit(solution)/shard_map/ppermute | solution.py:26
  62.6 2.1 %copy-start.14 = (f32[108,8,4,32]{0,3,1,2:T(8,128)S(1)}, f32[108,8,4,32]{0,3,1,2:T(8,128)}, u32[]{:S(2)}) copy-start(f32[108,8,4,32]{0,3,1,2:T(8,128)} %get-tuple-element.20) | copy-start | bytes 1327108
  73.5 1.7 %copy-start.16 = (f32[108,8,3,32]{0,3,1,2:T(8,128)S(1)}, f32[108,8,3,32]{0,3,1,2:T(8,128)}, u32[]{:S(2)}) copy-start(f32[108,8,3,32]{0,3,1,2:T(8,128)} %get-tuple-element.58) | copy-start | bytes 995332
  80.9 20.7 %collective-permute-start.6 = (f32[108,8,64]{0,2,1:T(8,128)}, f32[108,8,64]{0,2,1:T(8,128)}, u32[]{:S(2)}, u32[]{:S(2)}) collective-permute-start(f32[108,8,64]{0,2,1:T(8,128)} %pad_maximum_fusion.23), channel_id=1, source_target_pairs={{0,8},{8,16},{16,24},{24,32},{32,40},{40,48},{48,56},{56,64},{64,7... | collective-permute-start | bytes 663560 | tf_op jit(solution)/shard_map/ppermute | solution.py:24
  82.9 18.7 %collective-permute-start.7 = (f32[108,8,64]{0,2,1:T(8,128)}, f32[108,8,64]{0,2,1:T(8,128)}, u32[]{:S(2)}, u32[]{:S(2)}) collective-permute-start(f32[108,8,64]{0,2,1:T(8,128)} %pad_maximum_fusion.23), channel_id=1, source_target_pairs={{8,0},{16,8},{24,16},{32,24},{40,32},{48,40},{56,48},{64,56},{72,6... | collective-permute-start | bytes 663560 | tf_op jit(solution)/shard_map/ppermute | solution.py:26
  104.6 2.7 %copy-start.48 = (pred[8]{0:T(512)(128)(4,1)S(1)}, pred[8]{0:T(512)(128)(4,1)}, u32[]{:S(2)}) copy-start(pred[8]{0:T(512)(128)(4,1)} %copy-done.47) | copy-start | bytes 28
  104.6 2.7 %copy-start.52 = (f32[8]{0:T(128)S(1)}, f32[8]{0:T(128)}, u32[]{:S(2)}) copy-start(f32[8]{0:T(128)} %copy-done.51) | copy-start | bytes 100
  105.5 3.1 %copy-start.4 = (f32[108,8,4,32]{0,3,2,1:T(8,128)S(1)}, f32[108,8,4,32]{0,3,2,1:T(8,128)}, u32[]{:S(2)}) copy-start(f32[108,8,4,32]{0,3,2,1:T(8,128)} %copy.81) | copy-start | bytes 1327108
  105.5 3.1 %copy-start.5 = (f32[108,8,4,32]{0,3,2,1:T(8,128)S(1)}, f32[108,8,4,32]{0,3,2,1:T(8,128)}, u32[]{:S(2)}) copy-start(f32[108,8,4,32]{0,3,2,1:T(8,128)} %copy.93) | copy-start | bytes 1327108
  105.5 3.1 %copy-start.30 = (f32[8,128]{1,0:T(8,128)S(1)}, f32[8,128]{1,0:T(8,128)}, u32[]{:S(2)}) copy-start(f32[8,128]{1,0:T(8,128)} %copy-done.29) | copy-start | bytes 12292
  105.5 3.2 %copy-start.62 = (pred[108]{0:T(512)(128)(4,1)S(1)}, pred[108]{0:T(512)(128)(4,1)}, u32[]{:S(2)}) copy-start(pred[108]{0:T(512)(128)(4,1)} %get-tuple-element.94) | copy-start | bytes 328
  105.5 3.2 %copy-start.66 = (pred[108]{0:T(512)(128)(4,1)S(1)}, pred[108]{0:T(512)(128)(4,1)}, u32[]{:S(2)}) copy-start(pred[108]{0:T(512)(128)(4,1)} %get-tuple-element.95) | copy-start | bytes 328
  105.5 3.2 %copy-start.70 = (f32[108]{0:T(128)S(1)}, f32[108]{0:T(128)}, u32[]{:S(2)}) copy-start(f32[108]{0:T(128)} %get-tuple-element.96) | copy-start | bytes 1300
  105.5 3.2 %copy-start.74 = (f32[108]{0:T(128)S(1)}, f32[108]{0:T(128)}, u32[]{:S(2)}) copy-start(f32[108]{0:T(128)} %get-tuple-element.97) | copy-start | bytes 1300
  107.4 1.3 copy-start.3
  115.2 13.9 %all-to-all-start = ((f32[108,8,128]{2,0,1:T(8,128)}), f32[108,8,128]{2,0,1:T(8,128)S(1)}, u32[]{:S(2)}, u32[]{:S(2)}) async-start(f32[108,8,128]{2,0,1:T(8,128)} %copy.99), calls=%async_computation | async-start | bytes 917504 | tf_op jit(solution)/shard_map/all_to_all | solution.py:108
  (55 other events, 47.7 us)
where the time goes:
time: 153 us; the launch traced here: 151 us
  local copies, waits for them, and re-layouts  49.5 us (32%)
  starting transfers between devices  40.9 us (27%)
  other arithmetic  37.8 us (25%)
  blocking collectives  11.9 us (8%)
  waiting for transfers between devices  9.6 us (6%)
    ppermute x4, starting transfers between devices, padded(): lax.ppermute(head, axis, [((i + 1) % count, i) for i in range(ends)])  27.4 us
    mul x4, other arithmetic, advect(): return moved * sea[None]  12.1 us
    gather x16, local copies, waits for them, and re-layouts, pick(): return jnp.take(rows, safe_index, axis=1) * valid[None, :, None]  12 us
    all_to_all x1, blocking collectives, body(): lax.all_to_all(gathered, 'spec', split_axis=0, concat_axis=1, tiled=True)  11.9 us
    unnamed x157, local copies, waits for them, and re-layouts  10.9 us
    all_to_all x1, waiting for transfers between devices, body(): lax.all_to_all(flat, 'spec', split_axis=1, concat_axis=0, tiled=True)  9.58 us
    ppermute x4, starting transfers between devices, padded(): lax.ppermute(tail, axis, [(i, (i + 1) % count) for i in range(ends)])  9.21 us
    all_to_all x1, starting transfers between devices, body(): lax.all_to_all(flat, 'spec', split_axis=1, concat_axis=0, tiled=True)  4.3 us
  transfers between devices with their start and end apart: 9, of which 1 were waited for; matrix products, arithmetic and copies ran while one was open for 20% of the time, Pallas kernels for 0%

commit v1 on v0

v1 whole, which is shorter than its diff:
```python
import functools
import math

import jax
import jax.numpy as jnp
import numpy as np
from jax import lax
from jax.experimental import pallas as pl
from jax.experimental.pallas import tpu as pltpu
from jax.sharding import PartitionSpec as P

NDIR = 36
ROWS = 4
COLS = 32
SUBSTEPS = 4
SOURCE_ITERS = 3
QUAD = 9
POINTS = ROWS * COLS
MESH = pl.DeviceIdType.MESH

ANGLE = (np.arange(NDIR) + 0.5) * (2.0 * math.pi / NDIR)


def table_pick(index, values):
    out = jnp.float32(values[0])
    for k in range(1, len(values)):
        out = jnp.where(index == k, jnp.float32(values[k]), out)
    return out


def take_rows(x, index):
    return jnp.take_along_axis(x, index, axis=0)


def take_lanes(x, index):
    return jnp.take_along_axis(x, index, axis=1)


def kernel(
    nt, ns, nf,
    spectra, speed_hbm, dir_hbm, mask_hbm, nb_hbm, out,
    own, halo, nb, small_f, small_i, aux_out, aux_in, grow, part, moments,
    load_sem, small_sem, aux_send, aux_recv, halo_send, halo_recv, mom_send, mom_recv, out_sem,
):
    tile = lax.axis_index("tile")
    spec = lax.axis_index("spec")
    above, beneath = lax.rem(tile + nt - 1, nt), lax.rem(tile + 1, nt)
    tiles_dev = own.shape[1]
    comps = nf * NDIR
    total_comps = comps * ns
    half = NDIR // 2

    barrier = pltpu.get_barrier_semaphore()
    for other in (above, beneath):
        pl.semaphore_signal(barrier, inc=1, device_id={"tile": other}, device_id_type=MESH)
    for k in range(1, ns):
        pl.semaphore_signal(
            barrier, inc=1, device_id={"spec": lax.rem(spec + k, ns)}, device_id_type=MESH
        )

    small = [
        pltpu.make_async_copy(nb_hbm, nb, small_sem.at[0]),
        pltpu.make_async_copy(mask_hbm, small_i, small_sem.at[1]),
        pltpu.make_async_copy(speed_hbm, small_f.at[0], small_sem.at[2]),
        pltpu.make_async_copy(dir_hbm, small_f.at[1], small_sem.at[3]),
    ]
    for copy in small:
        copy.start()
    loads = [
        pltpu.make_async_copy(
            spectra.at[pl.ds(lf * NDIR, NDIR)], own.at[pl.ds(lf * NDIR, NDIR)], load_sem.at[lf]
        )
        for lf in range(nf)
    ]
    for copy in loads:
        copy.start()

    shape = (tiles_dev, POINTS)
    lane = lax.broadcasted_iota(jnp.int32, shape, 1)
    row_of = lane // COLS
    col_of = lane - row_of * COLS
    sublane = lax.broadcasted_iota(jnp.int32, shape, 0)
    small[0].wait()
    ids = nb[...]
    base = tile * tiles_dev

    def spread(k):
        return jnp.broadcast_to(ids[:, k : k + 1], shape)

    def local(wide, first):
        return jnp.clip(wide - first, 0, tiles_dev - 1)

    north_id, south_id, west_id, east_id = [spread(k) for k in range(4)]
    north_at, south_at = local(north_id, base - tiles_dev), local(south_id, base + tiles_dev)
    west_at, east_at = local(west_id, base), local(east_id, base)
    small[1].wait()
    mask_i = small_i[...]
    for way, place in ((0, south_at), (1, north_at)):
        aux_out[way, 0] = mask_i
        aux_out[way, 1] = jnp.where(west_id >= 0, take_rows(place, west_at), -1)
        aux_out[way, 2] = jnp.where(east_id >= 0, take_rows(place, east_at), -1)

    pl.semaphore_wait(barrier, 2 + ns - 1)

    sends = []
    for way, other in ((0, beneath), (1, above)):
        sends.append(
            pltpu.make_async_remote_copy(
                src_ref=aux_out.at[way], dst_ref=aux_in.at[way],
                send_sem=aux_send.at[way], recv_sem=aux_recv.at[way],
                device_id={"tile": other}, device_id_type=MESH,
            )
        )
    for lf in range(nf):
        for q in range(2):
            for way, other in ((0, beneath), (1, above)):
                run = pl.ds(lf * NDIR + way * half + q * QUAD, QUAD)
                slot = lf * 4 + way * 2 + q
                sends.append(
                    pltpu.make_async_remote_copy(
                        src_ref=spectra.at[run], dst_ref=halo.at[run],
                        send_sem=halo_send.at[slot], recv_sem=halo_recv.at[slot],
                        device_id={"tile": other}, device_id_type=MESH,
                    )
                )
    for copy in sends:
        copy.start()

    small[2].wait()
    small[3].wait()
    scaled = small_f[0] * jnp.float32(0.2 * 0.03)
    cos_w, sin_w = jnp.cos(small_f[1]), jnp.sin(small_f[1])
    for d in range(NDIR):
        cosine = cos_w * jnp.float32(math.cos(ANGLE[d])) + sin_w * jnp.float32(math.sin(ANGLE[d]))
        grow[d] = scaled * jnp.maximum(cosine, 0.0)

    mask = mask_i.astype(jnp.float32)
    one = jnp.float32(1.0)
    zero = jnp.float32(0.0)

    def sideways(at, valid, edge):
        return (
            jnp.where(col_of == edge, at, sublane),
            jnp.where((col_of == COLS - 1 - edge) & jnp.logical_not(valid), zero, one),
        )

    from_west = row_of * COLS + lax.rem(col_of + COLS - 1, COLS)
    from_east = row_of * COLS + lax.rem(col_of + 1, COLS)
    side_own = (
        sideways(west_at, west_id >= 0, COLS - 1),
        sideways(east_at, east_id >= 0, 0),
    )
    lanes_of = (from_west, from_east)
    ratio_spec = table_pick(spec, [1.1 ** (nf * s) for s in range(ns)])
    ratio_of = [ratio_spec * jnp.float32(1.1**lf) for lf in range(nf)]

    aux_waits = sends[:2]
    for copy in aux_waits:
        copy.wait_recv()
    halo_setup = []
    for way, (place, ident) in enumerate(((north_at, north_id), (south_at, south_id))):
        hmask = jnp.where(ident >= 0, take_rows(aux_in[way, 0], place), 0).astype(jnp.float32)
        sides = []
        for k, edge in ((1, COLS - 1), (2, 0)):
            at = take_rows(aux_in[way, k], place)
            sides.append(sideways(jnp.maximum(at, 0), at >= 0, edge))
        halo_setup.append((hmask, sides))

    def advance_freq(lf, carry):
        first, second = carry
        ratio = jnp.float32(ratio_of[0])
        for k in range(1, nf):
            ratio = jnp.where(lf == k, ratio_of[k], ratio)
        speed = jnp.float32(0.65) / ratio
        subtotal = jnp.zeros(shape, jnp.float32)
        start = lf * NDIR
        pltpu.make_async_copy(
            spectra.at[pl.ds(start, NDIR)], own.at[pl.ds(start, NDIR)], load_sem.at[lf]
        ).wait()
        for q, way, side in ((0, 0, 0), (0, 1, 1), (1, 0, 1), (1, 1, 0)):
            run = pl.ds(start + way * half + q * QUAD, QUAD)
            slot = lf * 4 + way * 2 + q
            pltpu.make_async_remote_copy(
                src_ref=spectra.at[run], dst_ref=halo.at[run],
                send_sem=halo_send.at[slot], recv_sem=halo_recv.at[slot],
                device_id={"tile": beneath if way == 0 else above}, device_id_type=MESH,
            ).wait_recv()
            place = north_at if way == 0 else south_at
            inner = ROWS - 1 if way == 0 else 0
            turn = COLS if way == 0 else POINTS - COLS
            rim = row_of == inner
            hmask, hsides = halo_setup[way]
            pull, keep = side_own[side]
            hpull, hkeep = hsides[side]
            lanes = lanes_of[side]
            for i in range(QUAD):
                d = way * half + q * QUAD + i
                ax = speed * jnp.float32(abs(math.cos(ANGLE[d])))
                ay = speed * jnp.float32(abs(math.sin(ANGLE[d])))
                rest = one - ax - ay
                kx, hkx = keep * ax, hkeep * ax
                x = own[start + d] * mask
                h = take_rows(halo[start + d], place) * hmask
                for step in range(SUBSTEPS):
                    side_x = take_lanes(take_rows(x, pull), lanes)
                    side_y = pltpu.roll(jnp.where(rim, h, x), turn, 1)
                    x = (rest * x + kx * side_x + ay * side_y) * mask
                    if step < SUBSTEPS - 1:
                        side_x = take_lanes(take_rows(h, hpull), lanes)
                        side_y = pltpu.roll(h, turn, 1)
                        h = (rest * h + hkx * side_x + ay * side_y) * hmask
                own[start + d] = x
                subtotal = subtotal + x
        weighted = ratio * subtotal
        return first + weighted, second + ratio * weighted

    empty = jnp.zeros(shape, jnp.float32)
    first, second = lax.fori_loop(0, nf, advance_freq, (empty, empty))

    chunk = NDIR // 3
    for step in range(SOURCE_ITERS):
        part[step, 0] = first
        part[step, 1] = second
        passes = []
        for k in range(1, ns):
            passes.append(
                pltpu.make_async_remote_copy(
                    src_ref=part.at[step], dst_ref=moments.at[step, k - 1],
                    send_sem=mom_send.at[step, k - 1], recv_sem=mom_recv.at[step, k - 1],
                    device_id={"spec": lax.rem(spec + k, ns)}, device_id_type=MESH,
                )
            )
        for copy in passes:
            copy.start()
        sends.extend(passes)
        for k in range(1, ns):
            passes[k - 1].wait_recv()
            first = first + moments[step, k - 1, 0]
            second = second + moments[step, k - 1, 1]
        first = first * jnp.float32(1.0 / total_comps)
        second = second * jnp.float32(1.0 / total_comps)
        mean_ratio = (second + 0.1) / (first + 0.1)
        damping = jnp.float32(0.2 * 0.25) * first / (mean_ratio * mean_ratio)
        damp = [damping * (ratio * ratio) for ratio in ratio_of]
        root = [ratio_spec_root * jnp.float32(math.sqrt(1.1**lf)) for lf in range(nf)
                for ratio_spec_root in (table_pick(spec, [math.sqrt(1.1 ** (nf * s)) for s in range(ns)]),)]
        limit = [jnp.float32(0.08) / ratio for ratio in ratio_of]

        def relax(j, sums):
            sums = list(sums)
            for i in range(chunk):
                d = j * chunk + i
                g = grow[d]
                for lf in range(nf):
                    x = own[lf * NDIR + d]
                    change = (g * root[lf] - damp[lf]) * x
                    change = jnp.minimum(jnp.maximum(change, -limit[lf]), limit[lf])
                    x = jnp.maximum(x + change, 0.0) * mask
                    own[lf * NDIR + d] = x
                    sums[lf] = sums[lf] + x
            if step == SOURCE_ITERS - 1:
                for lf in range(nf):
                    run = pl.ds(lf * NDIR + j * chunk, chunk)
                    pltpu.make_async_copy(own.at[run], out.at[run], out_sem.at[j, lf]).start()
            return tuple(sums)

        sums = lax.fori_loop(0, NDIR // chunk, relax, (empty,) * nf)
        first = sum(ratio * s for ratio, s in zip(ratio_of, sums))
        second = sum(ratio * ratio * s for ratio, s in zip(ratio_of, sums))

    for j in range(NDIR // chunk):
        for lf in range(nf):
            run = pl.ds(lf * NDIR + j * chunk, chunk)
            pltpu.make_async_copy(own.at[run], out.at[run], out_sem.at[j, lf]).wait()
    for copy in sends:
        copy.wait_send()


def body(nt, ns, spectra, wind_speed, wind_dir, sea_mask, neighbours):
    comps, tiles_dev, points = spectra.shape
    nf = comps // NDIR
    anywhere = pl.BlockSpec(memory_space=pl.ANY)
    dma = pltpu.SemaphoreType.DMA
    return pl.pallas_call(
        functools.partial(kernel, nt, ns, nf),
        out_shape=jax.ShapeDtypeStruct(spectra.shape, jnp.float32),
        in_specs=[anywhere] * 5,
        out_specs=anywhere,
        scratch_shapes=[
            pltpu.VMEM((comps, tiles_dev, points), jnp.float32),
            pltpu.VMEM((comps, tiles_dev, points), jnp.float32),
            pltpu.VMEM((tiles_dev, 4), jnp.int32),
            pltpu.VMEM((2, tiles_dev, points), jnp.float32),
            pltpu.VMEM((tiles_dev, points), jnp.int32),
            pltpu.VMEM((2, 3, tiles_dev, points), jnp.int32),
            pltpu.VMEM((2, 3, tiles_dev, points), jnp.int32),
            pltpu.VMEM((NDIR, tiles_dev, points), jnp.float32),
            pltpu.VMEM((SOURCE_ITERS, 2, tiles_dev, points), jnp.float32),
            pltpu.VMEM((SOURCE_ITERS, ns - 1, 2, tiles_dev, points), jnp.float32),
            dma((nf,)),
            dma((4,)),
            dma((2,)),
            dma((2,)),
            dma((nf * 4,)),
            dma((nf * 4,)),
            dma((SOURCE_ITERS, ns - 1)),
            dma((SOURCE_ITERS, ns - 1)),
            dma((3, nf)),
        ],
        compiler_params=pltpu.CompilerParams(
            collective_id=0, has_side_effects=True, vmem_limit_bytes=16 * 1024 * 1024
        ),
    )(spectra, wind_speed, wind_dir, sea_mask, neighbours)


def solution(mesh):
    placed = (
        P("spec", "tile", None),
        P("tile", None),
        P("tile", None),
        P("tile", None),
        P("tile", None),
    )
    return jax.shard_map(
        functools.partial(body, mesh.shape["tile"], mesh.shape["spec"]),
        mesh=mesh, in_specs=placed, out_specs=P("spec", "tile", None), check_vma=False,
    )
```

time: 153 us -> 44.1 us (0.29)
  the two profiles are of different devices: /device:TPU:256 before, /device:TPU:1 now
where the time goes in v1:
time: 44.1 us; the launch traced here: 43.8 us
  Pallas kernels  39.9 us (90%)
  local copies, waits for them, and re-layouts  3.92 us (9%)
    pallas_call x1, Pallas kernels, body(): pl.pallas_call(functools.partial(kernel, nt, ns, nf), out_shape=jax.Shape...  39.9 us
    unnamed x10, local copies, waits for them, and re-layouts  3.92 us

profile of v1, /device:TPU:1, one launch (start us, length us, event | category | flops | bytes accessed | tf_op | source)
XLA Modules:
  0.0 43.8 jit_solution(1415922805257228332)
XLA Ops:
  0.0 0.0 copy-start.1
  0.0 0.8 %copy.6.nb_hbm = s32[8,4]{1,0:T(8,128)S(1)} copy(s32[8,4]{0,1:T(4,128)} %param.9) | data formatting | bytes 256 | tf_op args[4]
  0.8 0.0 copy-done.1
  0.8 0.0 copy-start
  0.8 1.0 %copy-done = f32[108,8,128]{2,1,0:T(8,128)S(1)} copy-done((f32[108,8,128]{2,1,0:T(8,128)S(1)}, f32[108,8,128]{2,1,0:T(8,128)}, u32[]{:S(2)}) %copy-start) | copy-done | bytes 442392
  1.8 0.0 copy-start.2
  1.8 0.7 %copy-done.2 = f32[8,128]{1,0:T(8,128)S(1)} copy-done((f32[8,128]{1,0:T(8,128)S(1)}, f32[8,128]{1,0:T(8,128)}, u32[]{:S(2)}) %copy-start.2) | copy-done | bytes 4120
  2.5 0.0 copy-start.3
  2.5 0.7 %copy-done.3 = s32[8,128]{1,0:T(8,128)S(1)} copy-done((s32[8,128]{1,0:T(8,128)S(1)}, s32[8,128]{1,0:T(8,128)}, u32[]{:S(2)}) %copy-start.3) | copy-done | bytes 4120
  3.2 39.9 %shard_map.55 = f32[108,8,128]{2,1,0:T(8,128)S(1)} custom-call(f32[108,8,128]{2,1,0:T(8,128)S(1)} %copy-done, f32[8,128]{1,0:T(8,128)S(1)} %copy-done.1, f32[8,128]{1,0:T(8,128)S(1)} %copy-done.2, s32[8,128]{1,0:T(8,128)S(1)} %copy-done.3, s32[8,4]{1,0:T(8,128)S(1)} %copy.6.nb_hbm), custom_call_target="tpu_custom_call" | custom-call | tf_op jit(solution)/shard_map/pallas_call | solution.py:284
  43.0 0.8 %copy.8 = f32[108,8,128]{2,1,0:T(8,128)} copy(f32[108,8,128]{2,1,0:T(8,128)S(1)} %shard_map.55) | data formatting | bytes 884736
Async XLA Ops:
  0.0 0.8 %copy-start.1 = (f32[8,128]{1,0:T(8,128)S(1)}, f32[8,128]{1,0:T(8,128)}, u32[]{:S(2)}) copy-start(f32[8,128]{1,0:T(8,128)} %speed_hbm.1) | copy-start | bytes 12292
  0.8 1.0 %copy-start = (f32[108,8,128]{2,1,0:T(8,128)S(1)}, f32[108,8,128]{2,1,0:T(8,128)}, u32[]{:S(2)}) copy-start(f32[108,8,128]{2,1,0:T(8,128)} %spectra.1) | copy-start | bytes 1327108
  1.8 0.7 %copy-start.2 = (f32[8,128]{1,0:T(8,128)S(1)}, f32[8,128]{1,0:T(8,128)}, u32[]{:S(2)}) copy-start(f32[8,128]{1,0:T(8,128)} %dir_hbm.1) | copy-start | bytes 12292
  2.5 0.7 %copy-start.3 = (s32[8,128]{1,0:T(8,128)S(1)}, s32[8,128]{1,0:T(8,128)}, u32[]{:S(2)}) copy-start(s32[8,128]{1,0:T(8,128)} %mask_hbm.1) | copy-start | bytes 12292

commit v2 on v1

v2 whole, which is shorter than its diff:
```python
import functools
import math

import jax
import jax.numpy as jnp
import numpy as np
from jax import lax
from jax.experimental import pallas as pl
from jax.experimental.pallas import tpu as pltpu
from jax.sharding import PartitionSpec as P

NDIR = 36
ROWS = 4
COLS = 32
SUBSTEPS = 4
SOURCE_ITERS = 3
QUAD = 9
POINTS = ROWS * COLS
MESH = pl.DeviceIdType.MESH

ANGLE = (np.arange(NDIR) + 0.5) * (2.0 * math.pi / NDIR)


def table_pick(index, values):
    out = jnp.float32(values[0])
    for k in range(1, len(values)):
        out = jnp.where(index == k, jnp.float32(values[k]), out)
    return out


def table_rows(row, values):
    out = jnp.full(row.shape, values[0], jnp.float32)
    for k in range(1, len(values)):
        out = jnp.where(row == k, jnp.float32(values[k]), out)
    return out


def take_rows(x, index):
    return jnp.take_along_axis(x, index, axis=0)


def take_lanes(x, index):
    return jnp.take_along_axis(x, index, axis=1)


def kernel(
    nt, ns, nf,
    spectra, speed_hbm, dir_hbm, mask_hbm, nb_hbm, own,
    halo, nb, small_f, small_i, aux_out, aux_in, grow, grow_row, gathered, q_out, q_in,
    index_t, factor_t,
    load_sem, small_sem, aux_send, aux_recv, halo_send, halo_recv,
    share_send, share_recv, share_own, q_send, q_recv,
):
    tile = lax.axis_index("tile")
    spec = lax.axis_index("spec")
    above, beneath = jnp.maximum(tile - 1, 0), jnp.minimum(tile + 1, nt - 1)
    tiles_dev = own.shape[1]
    comps = nf * NDIR
    total_comps = comps * ns
    blocks = nf * ns // 8
    half = NDIR // 2

    barrier = pltpu.get_barrier_semaphore()
    ways = ((0, beneath, tile < nt - 1), (1, above, tile > 0))
    for way, other, there in ways:

        @pl.when(there)
        def _():
            pl.semaphore_signal(barrier, inc=1, device_id={"tile": other}, device_id_type=MESH)

    for k in range(1, ns):
        pl.semaphore_signal(
            barrier, inc=1, device_id={"spec": lax.rem(spec + k, ns)}, device_id_type=MESH
        )

    small = [
        pltpu.make_async_copy(nb_hbm, nb, small_sem.at[0]),
        pltpu.make_async_copy(mask_hbm, small_i, small_sem.at[1]),
        pltpu.make_async_copy(speed_hbm, small_f.at[0], small_sem.at[2]),
        pltpu.make_async_copy(dir_hbm, small_f.at[1], small_sem.at[3]),
    ]
    for copy in small:
        copy.start()

    def own_copy(lf):
        run = pl.ds(lf * NDIR, NDIR)
        return pltpu.make_async_copy(spectra.at[run], own.at[run], load_sem.at[lf])

    for lf in range(nf):
        own_copy(lf).start()

    def aux_copy(way, other):
        return pltpu.make_async_remote_copy(
            src_ref=aux_out.at[way], dst_ref=aux_in.at[way],
            send_sem=aux_send.at[way], recv_sem=aux_recv.at[way],
            device_id={"tile": other}, device_id_type=MESH,
        )

    def halo_copy(lf, way, other):
        run = pl.ds(lf * NDIR + way * half, half)
        return pltpu.make_async_remote_copy(
            src_ref=spectra.at[run], dst_ref=halo.at[run],
            send_sem=halo_send.at[lf, way], recv_sem=halo_recv.at[lf, way],
            device_id={"tile": other}, device_id_type=MESH,
        )

    pl.semaphore_wait(
        barrier, ns - 1 + (tile > 0).astype(jnp.int32) + (tile < nt - 1).astype(jnp.int32)
    )
    comes = (tile > 0, tile < nt - 1)
    for way, other, there in ways:

        @pl.when(there)
        def _():
            halo_copy(0, way, other).start()

    shape = (tiles_dev, POINTS)
    lane = lax.broadcasted_iota(jnp.int32, shape, 1)
    row_of = lane // COLS
    col_of = lane - row_of * COLS
    sublane = lax.broadcasted_iota(jnp.int32, shape, 0)
    small[0].wait()
    base = tile * tiles_dev

    def spread(k):
        wide = jnp.full(shape, nb[k, 0], jnp.int32)
        for s in range(1, tiles_dev):
            wide = jnp.where(sublane == s, nb[k, s], wide)
        return wide

    def local(wide, first):
        return jnp.clip(wide - first, 0, tiles_dev - 1)

    north_id, south_id, west_id, east_id = [spread(k) for k in range(4)]
    north_at, south_at = local(north_id, base - tiles_dev), local(south_id, base + tiles_dev)
    west_at, east_at = local(west_id, base), local(east_id, base)
    small[1].wait()
    mask_i = small_i[...]
    for way, place in ((0, south_at), (1, north_at)):
        aux_out[way, 0] = mask_i
        aux_out[way, 1] = jnp.where(west_id >= 0, take_rows(place, west_at), -1)
        aux_out[way, 2] = jnp.where(east_id >= 0, take_rows(place, east_at), -1)

    for way, other, there in ways:

        @pl.when(there)
        def _():
            aux_copy(way, other).start()

        @pl.when(jnp.logical_not(comes[way]))
        def _():
            aux_in[way] = jnp.zeros(aux_in.shape[1:], jnp.int32)
            for lf in range(nf):
                run = pl.ds(lf * NDIR + way * half, half)
                halo[run] = jnp.zeros((half,) + shape, jnp.float32)

    def next_halo(lf):
        for way, other, there in ways:

            @pl.when(there)
            def _():
                halo_copy(lf - 1, way, other).wait_send()
                halo_copy(lf, way, other).start()

    small[2].wait()
    small[3].wait()
    scaled = small_f[0] * jnp.float32(0.2 * 0.03)
    small_f[2] = jnp.cos(small_f[1])
    small_f[3] = jnp.sin(small_f[1])
    small_f[4] = mask_i.astype(jnp.float32)
    small_f[5] = scaled

    def mine(k):
        return jnp.broadcast_to(small_f[k, pl.ds(spec, 1), :], (8, POINTS))

    for target, cos_w, sin_w, scale in (
        (grow, small_f[2], small_f[3], scaled), (grow_row, mine(2), mine(3), mine(5))
    ):
        for d in range(NDIR):
            cosine = cos_w * jnp.float32(math.cos(ANGLE[d]))
            cosine = cosine + sin_w * jnp.float32(math.sin(ANGLE[d]))
            target[d] = scale * jnp.maximum(cosine, 0.0)
    for lf in range(1, nf):
        next_halo(lf)

    mask = mask_i.astype(jnp.float32)
    one = jnp.float32(1.0)
    zero = jnp.float32(0.0)
    empty = jnp.zeros(shape, jnp.float32)
    ratio_spec = table_pick(spec, [1.1 ** (nf * s) for s in range(ns)])
    ratio_of = [ratio_spec * jnp.float32(1.1**lf) for lf in range(nf)]

    def sideways(at, valid, edge):
        return (
            jnp.where(col_of == edge, at, sublane),
            jnp.where((col_of == COLS - 1 - edge) & jnp.logical_not(valid), zero, one),
        )

    lanes_of = (
        row_of * COLS + lax.rem(col_of + COLS - 1, COLS),
        row_of * COLS + lax.rem(col_of + 1, COLS),
    )
    side_own = (
        sideways(west_at, west_id >= 0, COLS - 1),
        sideways(east_at, east_id >= 0, 0),
    )
    for way, place, ident, turn in (
        (0, north_at, north_id, POINTS - COLS), (1, south_at, south_id, COLS)
    ):

        @pl.when(comes[way])
        def _():
            aux_copy(way, ways[way][1]).wait_recv()

        factor_t[way, 4] = jnp.where(ident >= 0, take_rows(aux_in[way, 0], place), 0).astype(
            jnp.float32
        )
        index_t[way, 6] = place
        index_t[way, 7] = lax.rem(lane + turn, POINTS)
        for q in range(2):
            side = way if q == 0 else 1 - way
            pull, keep = side_own[side]
            at = take_rows(aux_in[way, 1 + side], place)
            hpull, hkeep = sideways(jnp.maximum(at, 0), at >= 0, COLS - 1 if side == 0 else 0)
            index_t[way, q], index_t[way, 2 + q], index_t[way, 4 + q] = pull, hpull, lanes_of[side]
            factor_t[way, q], factor_t[way, 2 + q] = keep, hkeep

    chunk = NDIR // 3
    order = sorted(range(1, ns), key=lambda k: -min(k // 2, (ns - k) // 2))

    def peer(k):
        return lax.rem(spec + k, ns)

    def share_copy(lf, k):
        return pltpu.make_async_remote_copy(
            src_ref=own.at[pl.ds(lf * NDIR, NDIR), peer(k)],
            dst_ref=gathered.at[:, spec * nf + lf],
            send_sem=share_send.at[lf, k - 1], recv_sem=share_recv.at[lf, k - 1],
            device_id={"spec": peer(k)}, device_id_type=MESH,
        )

    def share_local(lf):
        return pltpu.make_async_copy(
            own.at[pl.ds(lf * NDIR, NDIR), spec], gathered.at[:, spec * nf + lf], share_own.at[lf]
        )

    def q_copy(k):
        return pltpu.make_async_remote_copy(
            src_ref=q_out.at[pl.ds(0, SOURCE_ITERS)], dst_ref=q_in.at[:, spec],
            send_sem=q_send.at[k - 1], recv_sem=q_recv.at[k - 1],
            device_id={"spec": peer(k)}, device_id_type=MESH,
        )

    swap = (tile > 0).astype(jnp.int32)

    def advance(group, carry):
        lf = group // 2
        way = lax.rem(group + swap, 2)
        ratio = jnp.float32(ratio_of[0])
        for k in range(1, nf):
            ratio = jnp.where(lf == k, ratio_of[k], ratio)
        speed = jnp.float32(0.65) / ratio
        start = lf * NDIR + way * half

        @pl.when(group == 2 * lf)
        def _():
            own_copy(lf).wait()

        for w in range(2):

            @pl.when((way == w) & comes[w])
            def _():
                halo_copy(lf, w, ways[w][1]).wait_recv()

        rim = row_of == (ROWS - 1) * (1 - way)
        place, turned = index_t[way, 6], index_t[way, 7]
        hmask = factor_t[way, 4]
        xs = [own[start + i] * mask for i in range(half)]
        hs = [take_rows(halo[start + i], place) * hmask for i in range(half)]
        coefs = []
        for i in range(half):
            ax = speed * jnp.float32(abs(math.cos(ANGLE[i])))
            ay = speed * jnp.float32(abs(math.sin(ANGLE[i])))
            coefs.append((ax, ay, one - ax - ay))
        for step in range(SUBSTEPS):
            for i in range(half):
                q = i // QUAD
                ax, ay, rest = coefs[i]
                lanes = index_t[way, 4 + q]
                x, h = xs[i], hs[i]
                side_x = take_lanes(take_rows(x, index_t[way, q]), lanes)
                side_y = take_lanes(jnp.where(rim, h, x), turned)
                xs[i] = (rest * x + (ax * factor_t[way, q]) * side_x + ay * side_y) * mask
                if step < SUBSTEPS - 1:
                    side_x = take_lanes(take_rows(h, index_t[way, 2 + q]), lanes)
                    side_y = take_lanes(h, turned)
                    hs[i] = (rest * h + (ax * factor_t[way, 2 + q]) * side_x + ay * side_y) * hmask
        for i in range(half):
            own[start + i] = xs[i]

        @pl.when(group == 2 * lf + 1)
        def _():
            for k in order:
                share_copy(lf, k).start()
            share_local(lf).start()

        return carry

    lax.fori_loop(0, 2 * nf, advance, 0)

    for lf in range(nf):
        share_local(lf).wait()
        for k in order:
            share_copy(lf, k).wait_recv()
    mask_row = mine(4)
    place8 = lax.broadcasted_iota(jnp.int32, (8, POINTS), 0)
    empty8 = jnp.zeros((8, POINTS), jnp.float32)
    freqs = [table_rows(place8, [1.1 ** (8 * b + s) for s in range(8)]) for b in range(blocks)]
    freq_root = [
        table_rows(place8, [math.sqrt(1.1 ** (8 * b + s)) for s in range(8)]) for b in range(blocks)
    ]
    freq_limit = [jnp.float32(0.08) / ratio for ratio in freqs]
    sums = [empty8] * blocks
    for d in range(NDIR):
        for b in range(blocks):
            sums[b] = sums[b] + gathered[d, 8 * b : 8 * b + 8, :]
    for step in range(SOURCE_ITERS):
        first = sum(ratio * t for ratio, t in zip(freqs, sums))
        second = sum(ratio * ratio * t for ratio, t in zip(freqs, sums))
        first = jnp.sum(first, axis=0, keepdims=True) * jnp.float32(1.0 / total_comps)
        second = jnp.sum(second, axis=0, keepdims=True) * jnp.float32(1.0 / total_comps)
        mean_ratio = (second + 0.1) / (first + 0.1)
        damping = jnp.float32(0.2 * 0.25) * first / (mean_ratio * mean_ratio)
        q_out[step : step + 1, :] = damping
        if step == SOURCE_ITERS - 1:
            break
        damping = jnp.broadcast_to(damping, (8, POINTS))
        damp = [damping * (ratio * ratio) for ratio in freqs]

        def relax(j, sums):
            sums = list(sums)
            for i in range(chunk):
                d = j * chunk + i
                g = grow_row[d]
                for b in range(blocks):
                    x = gathered[d, 8 * b : 8 * b + 8, :]
                    change = (g * freq_root[b] - damp[b]) * x
                    change = jnp.minimum(jnp.maximum(change, -freq_limit[b]), freq_limit[b])
                    x = jnp.maximum(x + change, 0.0) * mask_row
                    gathered[d, 8 * b : 8 * b + 8, :] = x
                    sums[b] = sums[b] + x
            return tuple(sums)

        sums = lax.fori_loop(0, NDIR // chunk, relax, (empty8,) * blocks)

    for k in order:
        q_copy(k).start()
    q_in[:, pl.ds(spec, 1), :] = q_out[0:SOURCE_ITERS, :].reshape(SOURCE_ITERS, 1, POINTS)
    root_spec = table_pick(spec, [math.sqrt(1.1 ** (nf * s)) for s in range(ns)])
    root = [root_spec * jnp.float32(math.sqrt(1.1**lf)) for lf in range(nf)]
    limit = [jnp.float32(0.08) / ratio for ratio in ratio_of]
    for lf in range(nf):
        for k in order:
            share_copy(lf, k).wait_send()
    for k in order:
        q_copy(k).wait_recv()
    dampings = [q_in[step] for step in range(SOURCE_ITERS)]
    damps = [[t * (ratio * ratio) for ratio in ratio_of] for t in dampings]

    def settle(j, carry):
        for i in range(chunk):
            d = j * chunk + i
            g = grow[d]
            for lf in range(nf):
                x = own[lf * NDIR + d]
                gain = g * root[lf]
                for step in range(SOURCE_ITERS):
                    change = (gain - damps[step][lf]) * x
                    change = jnp.minimum(jnp.maximum(change, -limit[lf]), limit[lf])
                    x = jnp.maximum(x + change, 0.0) * mask
                own[lf * NDIR + d] = x
        return carry

    lax.fori_loop(0, NDIR // chunk, settle, 0)

    for way, other, there in ways:

        @pl.when(there)
        def _():
            aux_copy(way, other).wait_send()
            halo_copy(nf - 1, way, other).wait_send()

    for k in order:
        q_copy(k).wait_send()


def body(nt, ns, spectra, wind_speed, wind_dir, sea_mask, neighbours):
    comps, tiles_dev, points = spectra.shape
    nf = comps // NDIR
    anywhere = pl.BlockSpec(memory_space=pl.ANY)
    dma = pltpu.SemaphoreType.DMA
    operands = [
        pltpu.with_memory_space_constraint(x, pltpu.HBM)
        for x in (spectra, wind_speed, wind_dir, sea_mask, neighbours.T)
    ]
    return pl.pallas_call(
        functools.partial(kernel, nt, ns, nf),
        out_shape=pltpu.VMEM(spectra.shape, jnp.float32),
        in_specs=[anywhere] * 5,
        out_specs=pl.BlockSpec(memory_space=pltpu.VMEM),
        scratch_shapes=[
            pltpu.VMEM((comps, tiles_dev, points), jnp.float32),
            pltpu.SMEM((4, tiles_dev), jnp.int32),
            pltpu.VMEM((6, tiles_dev, points), jnp.float32),
            pltpu.VMEM((tiles_dev, points), jnp.int32),
            pltpu.VMEM((2, 3, tiles_dev, points), jnp.int32),
            pltpu.VMEM((2, 3, tiles_dev, points), jnp.int32),
            pltpu.VMEM((NDIR, tiles_dev, points), jnp.float32),
            pltpu.VMEM((NDIR, 8, points), jnp.float32),
            pltpu.VMEM((NDIR, nf * ns, points), jnp.float32),
            pltpu.VMEM((8, points), jnp.float32),
            pltpu.VMEM((SOURCE_ITERS, tiles_dev, points), jnp.float32),
            pltpu.VMEM((2, 8, tiles_dev, points), jnp.int32),
            pltpu.VMEM((2, 5, tiles_dev, points), jnp.float32),
            dma((nf,)),
            dma((4,)),
            dma((2,)),
            dma((2,)),
            dma((nf, 2)),
            dma((nf, 2)),
            dma((nf, ns - 1)),
            dma((nf, ns - 1)),
            dma((nf,)),
            dma((ns - 1,)),
            dma((ns - 1,)),
        ],
        compiler_params=pltpu.CompilerParams(
            collective_id=0, has_side_effects=True, vmem_limit_bytes=16 * 1024 * 1024
        ),
    )(*operands)


def solution(mesh):
    placed = (
        P("spec", "tile", None),
        P("tile", None),
        P("tile", None),
        P("tile", None),
        P("tile", None),
    )
    return jax.shard_map(
        functools.partial(body, mesh.shape["tile"], mesh.shape["spec"]),
        mesh=mesh, in_specs=placed, out_specs=P("spec", "tile", None), check_vma=False,
    )
```

time: 44.1 us -> 30.1 us (0.68)
  Pallas kernels: 39.9 us -> 29.2 us
  local copies, waits for them, and re-layouts: 3.92 us -> 0.76 us
    pallas_call x1, Pallas kernels: 39.9 us -> 29.2 us  [body(): pl.pallas_call(functools.partial(kernel, nt, ns, nf), out_shape=pltpu.VME...]
    unnamed x10 -> x1, local copies, waits for them, and re-layouts: 3.92 us -> 0.76 us
where the time goes in v2:
time: 30.1 us; the launch traced here: 30 us
  Pallas kernels  29.2 us (97%)
  local copies, waits for them, and re-layouts  0.76 us (3%)
    pallas_call x1, Pallas kernels, body(): pl.pallas_call(functools.partial(kernel, nt, ns, nf), out_shape=pltpu.VME...  29.2 us
    unnamed x1, local copies, waits for them, and re-layouts  0.76 us

profile of v2, /device:TPU:1, one launch (start us, length us, event | category | flops | bytes accessed | tf_op | source)
XLA Modules:
  0.0 30.0 jit_solution(6180173985540557148)
XLA Ops:
  0.0 29.2 %shard_map.55 = f32[108,8,128]{2,1,0:T(8,128)S(1)} custom-call(f32[108,8,128]{2,1,0:T(8,128)} %spectra.1, f32[8,128]{1,0:T(8,128)} %speed_hbm.1, f32[8,128]{1,0:T(8,128)} %dir_hbm.1, s32[8,128]{1,0:T(8,128)} %mask_hbm.1, s32[4,8]{1,0:T(4,128)} %bitcast.1), custom_call_target="tpu_custom_call" | custom-call | tf_op jit(solution)/shard_map/pallas_call | solution.py:406
  29.2 0.8 %copy.7 = f32[108,8,128]{2,1,0:T(8,128)} copy(f32[108,8,128]{2,1,0:T(8,128)S(1)} %shard_map.55) | data formatting | bytes 884736

commit v3 on v2

--- a/solution.py
+++ b/solution.py
@@ -49,7 +49,7 @@
     halo, nb, small_f, small_i, aux_out, aux_in, grow, grow_row, gathered, q_out, q_in,
     index_t, factor_t,
     load_sem, small_sem, aux_send, aux_recv, halo_send, halo_recv,
-    share_send, share_recv, share_own, q_send, q_recv,
+    share_send, share_recv, share_own, q_send, q_recv, met,
 ):
     tile = lax.axis_index("tile")
     spec = lax.axis_index("spec")
@@ -60,6 +60,14 @@
     blocks = nf * ns // 8
     half = NDIR // 2
 
+    chips = ns // 2
+    around = lax.rem(spec, 2) * chips + spec // 2
+
+    def on_ring(offset):
+        v = lax.rem(around + offset, ns)
+        return lax.rem(v, chips) * 2 + v // chips
+
+    greeted = [on_ring(offset) for offset in (1, ns - 1, chips)]
     barrier = pltpu.get_barrier_semaphore()
     ways = ((0, beneath, tile < nt - 1), (1, above, tile > 0))
     for way, other, there in ways:
@@ -68,10 +76,8 @@
         def _():
             pl.semaphore_signal(barrier, inc=1, device_id={"tile": other}, device_id_type=MESH)
 
-    for k in range(1, ns):
-        pl.semaphore_signal(
-            barrier, inc=1, device_id={"spec": lax.rem(spec + k, ns)}, device_id_type=MESH
-        )
+    for other in greeted:
+        pl.semaphore_signal(barrier, inc=1, device_id={"spec": other}, device_id_type=MESH)
 
     small = [
         pltpu.make_async_copy(nb_hbm, nb, small_sem.at[0]),
@@ -105,7 +111,7 @@
         )
 
     pl.semaphore_wait(
-        barrier, ns - 1 + (tile > 0).astype(jnp.int32) + (tile < nt - 1).astype(jnp.int32)
+        barrier, len(greeted) + (tile > 0).astype(jnp.int32) + (tile < nt - 1).astype(jnp.int32)
     )
     comes = (tile > 0, tile < nt - 1)
     for way, other, there in ways:
@@ -113,6 +119,9 @@
         @pl.when(there)
         def _():
             halo_copy(0, way, other).start()
+
+    for other in greeted:
+        pl.semaphore_signal(met, inc=1, device_id={"spec": other}, device_id_type=MESH)
 
     shape = (tiles_dev, POINTS)
     lane = lax.broadcasted_iota(jnp.int32, shape, 1)
@@ -147,20 +156,21 @@
         def _():
             aux_copy(way, other).start()
 
+    for lf in range(1, nf):
+        for way, other, there in ways:
+
+            @pl.when(there)
+            def _():
+                halo_copy(lf, way, other).start()
+
+    for way, other, there in ways:
+
         @pl.when(jnp.logical_not(comes[way]))
         def _():
             aux_in[way] = jnp.zeros(aux_in.shape[1:], jnp.int32)
             for lf in range(nf):
                 run = pl.ds(lf * NDIR + way * half, half)
                 halo[run] = jnp.zeros((half,) + shape, jnp.float32)
-
-    def next_halo(lf):
-        for way, other, there in ways:
-
-            @pl.when(there)
-            def _():
-                halo_copy(lf - 1, way, other).wait_send()
-                halo_copy(lf, way, other).start()
 
     small[2].wait()
     small[3].wait()
@@ -176,12 +186,15 @@
     for target, cos_w, sin_w, scale in (
         (grow, small_f[2], small_f[3], scaled), (grow_row, mine(2), mine(3), mine(5))
     ):
-        for d in range(NDIR):
-            cosine = cos_w * jnp.float32(math.cos(ANGLE[d]))
-            cosine = cosine + sin_w * jnp.float32(math.sin(ANGLE[d]))
-            target[d] = scale * jnp.maximum(cosine, 0.0)
-    for lf in range(1, nf):
-        next_halo(lf)
+        along, across = scale * cos_w, scale * sin_w
+        for d in range(QUAD):
+            cos_d, sin_d = jnp.float32(math.cos(ANGLE[d])), jnp.float32(math.sin(ANGLE[d]))
+            ahead = along * cos_d + across * sin_d
+            aside = across * cos_d - along * sin_d
+            target[d] = jnp.maximum(ahead, 0.0)
+            target[QUAD + d] = jnp.maximum(aside, 0.0)
+            target[2 * QUAD + d] = jnp.maximum(-ahead, 0.0)
+            target[3 * QUAD + d] = jnp.maximum(-aside, 0.0)
 
     mask = mask_i.astype(jnp.float32)
     one = jnp.float32(1.0)
@@ -225,7 +238,7 @@
             index_t[way, q], index_t[way, 2 + q], index_t[way, 4 + q] = pull, hpull, lanes_of[side]
             factor_t[way, q], factor_t[way, 2 + q] = keep, hkeep
 
-    chunk = NDIR // 3
+    chunk = NDIR // 6
     order = sorted(range(1, ns), key=lambda k: -min(k // 2, (ns - k) // 2))
 
     def peer(k):
@@ -298,6 +311,10 @@
         for i in range(half):
             own[start + i] = xs[i]
 
+        @pl.when(group == 1)
+        def _():
+            pl.semaphore_wait(met, len(greeted))
+
         @pl.when(group == 2 * lf + 1)
         def _():
             for k in order:
@@ -308,10 +325,13 @@
 
     lax.fori_loop(0, 2 * nf, advance, 0)
 
-    for lf in range(nf):
+    def arrive(lf, carry):
         share_local(lf).wait()
         for k in order:
             share_copy(lf, k).wait_recv()
+        return carry
+
+    lax.fori_loop(0, nf, arrive, 0)
     mask_row = mine(4)
     place8 = lax.broadcasted_iota(jnp.int32, (8, POINTS), 0)
     empty8 = jnp.zeros((8, POINTS), jnp.float32)
@@ -320,10 +340,15 @@
         table_rows(place8, [math.sqrt(1.1 ** (8 * b + s)) for s in range(8)]) for b in range(blocks)
     ]
     freq_limit = [jnp.float32(0.08) / ratio for ratio in freqs]
-    sums = [empty8] * blocks
-    for d in range(NDIR):
-        for b in range(blocks):
-            sums[b] = sums[b] + gathered[d, 8 * b : 8 * b + 8, :]
+
+    def gather_sums(j, sums):
+        sums = list(sums)
+        for i in range(chunk):
+            for b in range(blocks):
+                sums[b] = sums[b] + gathered[j * chunk + i, 8 * b : 8 * b + 8, :]
+        return tuple(sums)
+
+    sums = lax.fori_loop(0, NDIR // chunk, gather_sums, (empty8,) * blocks)
     for step in range(SOURCE_ITERS):
         first = sum(ratio * t for ratio, t in zip(freqs, sums))
         second = sum(ratio * ratio * t for ratio, t in zip(freqs, sums))
@@ -359,9 +384,12 @@
     root_spec = table_pick(spec, [math.sqrt(1.1 ** (nf * s)) for s in range(ns)])
     root = [root_spec * jnp.float32(math.sqrt(1.1**lf)) for lf in range(nf)]
     limit = [jnp.float32(0.08) / ratio for ratio in ratio_of]
-    for lf in range(nf):
+    def left(lf, carry):
         for k in order:
             share_copy(lf, k).wait_send()
+        return carry
+
+    lax.fori_loop(0, nf, left, 0)
     for k in order:
         q_copy(k).wait_recv()
     dampings = [q_in[step] for step in range(SOURCE_ITERS)]
@@ -388,7 +416,8 @@
         @pl.when(there)
         def _():
             aux_copy(way, other).wait_send()
-            halo_copy(nf - 1, way, other).wait_send()
+            for lf in range(nf):
+                halo_copy(lf, way, other).wait_send()
 
     for k in order:
         q_copy(k).wait_send()
@@ -433,6 +462,7 @@
             dma((nf,)),
             dma((ns - 1,)),
             dma((ns - 1,)),
+            pltpu.SemaphoreType.REGULAR,
         ],
         compiler_params=pltpu.CompilerParams(
             collective_id=0, has_side_effects=True, vmem_limit_bytes=16 * 1024 * 1024

time: 30.1 us -> 28 us (0.930)
  Pallas kernels: 29.2 us -> 27.1 us
    pallas_call x1, Pallas kernels: 29.2 us -> 27.1 us  [body(): pl.pallas_call(functools.partial(kernel, nt, ns, nf), out_shape=pltpu.VME...]
where the time goes in v3:
time: 28 us; the launch traced here: 27.8 us
  Pallas kernels  27.1 us (97%)
  local copies, waits for them, and re-layouts  0.76 us (3%)
    pallas_call x1, Pallas kernels, body(): pl.pallas_call(functools.partial(kernel, nt, ns, nf), out_shape=pltpu.VME...  27.1 us
    unnamed x1, local copies, waits for them, and re-layouts  0.76 us

profile of v3, /device:TPU:1, one launch (start us, length us, event | category | flops | bytes accessed | tf_op | source)
XLA Modules:
  0.0 27.8 jit_solution(12296228657952917279)
XLA Ops:
  0.0 27.1 %shard_map.55 = f32[108,8,128]{2,1,0:T(8,128)S(1)} custom-call(f32[108,8,128]{2,1,0:T(8,128)} %spectra.1, f32[8,128]{1,0:T(8,128)} %speed_hbm.1, f32[8,128]{1,0:T(8,128)} %dir_hbm.1, s32[8,128]{1,0:T(8,128)} %mask_hbm.1, s32[4,8]{1,0:T(4,128)} %bitcast.1), custom_call_target="tpu_custom_call" | custom-call | tf_op jit(solution)/shard_map/pallas_call | solution.py:435
  27.1 0.8 %copy.7 = f32[108,8,128]{2,1,0:T(8,128)} copy(f32[108,8,128]{2,1,0:T(8,128)S(1)} %shard_map.55) | data formatting | bytes 884736

commit v4 on v3

--- a/solution.py
+++ b/solution.py
@@ -57,7 +57,7 @@
     tiles_dev = own.shape[1]
     comps = nf * NDIR
     total_comps = comps * ns
-    blocks = nf * ns // 8
+    blocks = nf
     half = NDIR // 2
 
     chips = ns // 2
@@ -106,7 +106,7 @@
         run = pl.ds(lf * NDIR + way * half, half)
         return pltpu.make_async_remote_copy(
             src_ref=spectra.at[run], dst_ref=halo.at[run],
-            send_sem=halo_send.at[lf, way], recv_sem=halo_recv.at[lf, way],
+            send_sem=halo_send.at[way], recv_sem=halo_recv.at[lf, way],
             device_id={"tile": other}, device_id_type=MESH,
         )
 
@@ -217,9 +217,10 @@
         sideways(west_at, west_id >= 0, COLS - 1),
         sideways(east_at, east_id >= 0, 0),
     )
-    for way, place, ident, turn in (
-        (0, north_at, north_id, POINTS - COLS), (1, south_at, south_id, COLS)
-    ):
+    def halo_tables(way):
+        place, ident, turn = (
+            (north_at, north_id, POINTS - COLS), (south_at, south_id, COLS)
+        )[way]
 
         @pl.when(comes[way])
         def _():
@@ -247,39 +248,56 @@
     def share_copy(lf, k):
         return pltpu.make_async_remote_copy(
             src_ref=own.at[pl.ds(lf * NDIR, NDIR), peer(k)],
-            dst_ref=gathered.at[:, spec * nf + lf],
-            send_sem=share_send.at[lf, k - 1], recv_sem=share_recv.at[lf, k - 1],
+            dst_ref=gathered.at[:, lf * ns + spec],
+            send_sem=share_send.at[lf], recv_sem=share_recv.at[lf],
             device_id={"spec": peer(k)}, device_id_type=MESH,
         )
 
     def share_local(lf):
         return pltpu.make_async_copy(
-            own.at[pl.ds(lf * NDIR, NDIR), spec], gathered.at[:, spec * nf + lf], share_own.at[lf]
+            own.at[pl.ds(lf * NDIR, NDIR), spec], gathered.at[:, lf * ns + spec], share_own.at[lf]
+        )
+
+    def share_all(sem):
+        return pltpu.make_async_copy(
+            gathered.at[:, pl.ds(0, ns - 1)], gathered.at[:, pl.ds(ns, ns - 1)], sem
+        )
+
+    def q_all(sem):
+        return pltpu.make_async_copy(
+            q_in.at[:, pl.ds(0, ns - 1)], q_in.at[:, pl.ds(0, ns - 1)], sem
         )
 
     def q_copy(k):
         return pltpu.make_async_remote_copy(
             src_ref=q_out.at[pl.ds(0, SOURCE_ITERS)], dst_ref=q_in.at[:, spec],
-            send_sem=q_send.at[k - 1], recv_sem=q_recv.at[k - 1],
+            send_sem=q_send.at[0], recv_sem=q_recv.at[0],
             device_id={"spec": peer(k)}, device_id_type=MESH,
         )
 
     swap = (tile > 0).astype(jnp.int32)
+    edge = (tile == 0) | (tile == nt - 1)
+    swap_edge = (tile == nt - 1).astype(jnp.int32)
 
     def advance(group, carry):
-        lf = group // 2
-        way = lax.rem(group + swap, 2)
+        lf = jnp.where(edge, lax.rem(group, nf), group // 2)
+        way = jnp.where(edge, lax.rem(group // nf + swap_edge, 2), lax.rem(group + swap, 2))
+        opens = jnp.where(edge, group < nf, lax.rem(group, 2) == 0)
         ratio = jnp.float32(ratio_of[0])
         for k in range(1, nf):
             ratio = jnp.where(lf == k, ratio_of[k], ratio)
         speed = jnp.float32(0.65) / ratio
         start = lf * NDIR + way * half
 
-        @pl.when(group == 2 * lf)
+        @pl.when(opens)
         def _():
             own_copy(lf).wait()
 
         for w in range(2):
+
+            @pl.when((way == w) & (lf == 0))
+            def _():
+                halo_tables(w)
 
             @pl.when((way == w) & comes[w])
             def _():
@@ -311,11 +329,11 @@
         for i in range(half):
             own[start + i] = xs[i]
 
-        @pl.when(group == 1)
+        @pl.when(jnp.logical_not(opens) & (lf == 0))
         def _():
             pl.semaphore_wait(met, len(greeted))
 
-        @pl.when(group == 2 * lf + 1)
+        @pl.when(jnp.logical_not(opens))
         def _():
             for k in order:
                 share_copy(lf, k).start()
@@ -325,30 +343,23 @@
 
     lax.fori_loop(0, 2 * nf, advance, 0)
 
-    def arrive(lf, carry):
-        share_local(lf).wait()
-        for k in order:
-            share_copy(lf, k).wait_recv()
-        return carry
-
-    lax.fori_loop(0, nf, arrive, 0)
     mask_row = mine(4)
     place8 = lax.broadcasted_iota(jnp.int32, (8, POINTS), 0)
     empty8 = jnp.zeros((8, POINTS), jnp.float32)
-    freqs = [table_rows(place8, [1.1 ** (8 * b + s) for s in range(8)]) for b in range(blocks)]
+    freqs = [table_rows(place8, [1.1 ** (nf * s + b) for s in range(ns)]) for b in range(blocks)]
     freq_root = [
-        table_rows(place8, [math.sqrt(1.1 ** (8 * b + s)) for s in range(8)]) for b in range(blocks)
+        table_rows(place8, [math.sqrt(1.1 ** (nf * s + b)) for s in range(ns)]) for b in range(blocks)
     ]
     freq_limit = [jnp.float32(0.08) / ratio for ratio in freqs]
 
-    def gather_sums(j, sums):
-        sums = list(sums)
-        for i in range(chunk):
-            for b in range(blocks):
-                sums[b] = sums[b] + gathered[j * chunk + i, 8 * b : 8 * b + 8, :]
-        return tuple(sums)
-
-    sums = lax.fori_loop(0, NDIR // chunk, gather_sums, (empty8,) * blocks)
+    sums = []
+    for b in range(blocks):
+        share_local(b).wait()
+        share_all(share_recv.at[b]).wait()
+        parts = [empty8] * 4
+        for d in range(NDIR):
+            parts[d % 4] = parts[d % 4] + gathered[d, 8 * b : 8 * b + 8, :]
+        sums.append((parts[0] + parts[1]) + (parts[2] + parts[3]))
     for step in range(SOURCE_ITERS):
         first = sum(ratio * t for ratio, t in zip(freqs, sums))
         second = sum(ratio * ratio * t for ratio, t in zip(freqs, sums))
@@ -384,14 +395,9 @@
     root_spec = table_pick(spec, [math.sqrt(1.1 ** (nf * s)) for s in range(ns)])
     root = [root_spec * jnp.float32(math.sqrt(1.1**lf)) for lf in range(nf)]
     limit = [jnp.float32(0.08) / ratio for ratio in ratio_of]
-    def left(lf, carry):
-        for k in order:
-            share_copy(lf, k).wait_send()
-        return carry
-
-    lax.fori_loop(0, nf, left, 0)
-    for k in order:
-        q_copy(k).wait_recv()
+    for lf in range(nf):
+        share_all(share_send.at[lf]).wait()
+    q_all(q_recv.at[0]).wait()
     dampings = [q_in[step] for step in range(SOURCE_ITERS)]
     damps = [[t * (ratio * ratio) for ratio in ratio_of] for t in dampings]
 
@@ -416,11 +422,11 @@
         @pl.when(there)
         def _():
             aux_copy(way, other).wait_send()
-            for lf in range(nf):
-                halo_copy(lf, way, other).wait_send()
-
-    for k in order:
-        q_copy(k).wait_send()
+            pltpu.make_async_copy(
+                halo.at[pl.ds(0, nf * half)], halo.at[pl.ds(nf * half, nf * half)], halo_send.at[way]
+            ).wait()
+
+    q_all(q_send.at[0]).wait()
 
 
 def body(nt, ns, spectra, wind_speed, wind_dir, sea_mask, neighbours):
@@ -455,13 +461,13 @@
             dma((4,)),
             dma((2,)),
             dma((2,)),
+            dma((2,)),
             dma((nf, 2)),
-            dma((nf, 2)),
-            dma((nf, ns - 1)),
-            dma((nf, ns - 1)),
             dma((nf,)),
-            dma((ns - 1,)),
-            dma((ns - 1,)),
+            dma((nf,)),
+            dma((nf,)),
+            dma((1,)),
+            dma((1,)),
             pltpu.SemaphoreType.REGULAR,
         ],
         compiler_params=pltpu.CompilerParams(

time: 28 us -> 26.5 us (0.946)
  Pallas kernels: 27.1 us -> 25.5 us
    pallas_call x1, Pallas kernels: 27.1 us -> 25.5 us  [body(): pl.pallas_call(functools.partial(kernel, nt, ns, nf), out_shape=pltpu.VME...]
where the time goes in v4:
time: 26.5 us; the launch traced here: 26.3 us
  Pallas kernels  25.5 us (96%)
  local copies, waits for them, and re-layouts  0.76 us (3%)
    pallas_call x1, Pallas kernels, body(): pl.pallas_call(functools.partial(kernel, nt, ns, nf), out_shape=pltpu.VME...  25.5 us
    unnamed x1, local copies, waits for them, and re-layouts  0.76 us

profile of v4, /device:TPU:1, one launch (start us, length us, event | category | flops | bytes accessed | tf_op | source)
XLA Modules:
  0.0 26.3 jit_solution(5074810177215134229)
XLA Ops:
  0.0 25.5 %shard_map.55 = f32[108,8,128]{2,1,0:T(8,128)S(1)} custom-call(f32[108,8,128]{2,1,0:T(8,128)} %spectra.1, f32[8,128]{1,0:T(8,128)} %speed_hbm.1, f32[8,128]{1,0:T(8,128)} %dir_hbm.1, s32[8,128]{1,0:T(8,128)} %mask_hbm.1, s32[4,8]{1,0:T(4,128)} %bitcast.1), custom_call_target="tpu_custom_call" | custom-call | tf_op jit(solution)/shard_map/pallas_call | solution.py:441
  25.5 0.8 %copy.7 = f32[108,8,128]{2,1,0:T(8,128)} copy(f32[108,8,128]{2,1,0:T(8,128)S(1)} %shard_map.55) | data formatting | bytes 884736

commit v5 on v4

--- a/solution.py
+++ b/solution.py
@@ -60,14 +60,11 @@
     blocks = nf
     half = NDIR // 2
 
-    chips = ns // 2
-    around = lax.rem(spec, 2) * chips + spec // 2
-
-    def on_ring(offset):
-        v = lax.rem(around + offset, ns)
-        return lax.rem(v, chips) * 2 + v // chips
-
-    greeted = [on_ring(offset) for offset in (1, ns - 1, chips)]
+    def ring_place(s):
+        return s // 4 * 4 + lax.rem(s, 2) * 2 + lax.rem(s // 2, 2)
+
+    around = ring_place(spec)
+    greeted = [ring_place(lax.rem(around + step, ns)) for step in (ns // 2, 1, ns - 1)]
     barrier = pltpu.get_barrier_semaphore()
     ways = ((0, beneath, tile < nt - 1), (1, above, tile > 0))
     for way, other, there in ways:
@@ -171,30 +168,6 @@
             for lf in range(nf):
                 run = pl.ds(lf * NDIR + way * half, half)
                 halo[run] = jnp.zeros((half,) + shape, jnp.float32)
-
-    small[2].wait()
-    small[3].wait()
-    scaled = small_f[0] * jnp.float32(0.2 * 0.03)
-    small_f[2] = jnp.cos(small_f[1])
-    small_f[3] = jnp.sin(small_f[1])
-    small_f[4] = mask_i.astype(jnp.float32)
-    small_f[5] = scaled
-
-    def mine(k):
-        return jnp.broadcast_to(small_f[k, pl.ds(spec, 1), :], (8, POINTS))
-
-    for target, cos_w, sin_w, scale in (
-        (grow, small_f[2], small_f[3], scaled), (grow_row, mine(2), mine(3), mine(5))
-    ):
-        along, across = scale * cos_w, scale * sin_w
-        for d in range(QUAD):
-            cos_d, sin_d = jnp.float32(math.cos(ANGLE[d])), jnp.float32(math.sin(ANGLE[d]))
-            ahead = along * cos_d + across * sin_d
-            aside = across * cos_d - along * sin_d
-            target[d] = jnp.maximum(ahead, 0.0)
-            target[QUAD + d] = jnp.maximum(aside, 0.0)
-            target[2 * QUAD + d] = jnp.maximum(-ahead, 0.0)
-            target[3 * QUAD + d] = jnp.maximum(-aside, 0.0)
 
     mask = mask_i.astype(jnp.float32)
     one = jnp.float32(1.0)
@@ -245,10 +218,10 @@
     def peer(k):
         return lax.rem(spec + k, ns)
 
-    def share_copy(lf, k):
+    def share_copy(lf, k, d=0, count=NDIR):
         return pltpu.make_async_remote_copy(
-            src_ref=own.at[pl.ds(lf * NDIR, NDIR), peer(k)],
-            dst_ref=gathered.at[:, lf * ns + spec],
+            src_ref=own.at[pl.ds(lf * NDIR + d, count), peer(k)],
+            dst_ref=gathered.at[pl.ds(d, count), lf * ns + spec],
             send_sem=share_send.at[lf], recv_sem=share_recv.at[lf],
             device_id={"spec": peer(k)}, device_id_type=MESH,
         )
@@ -276,12 +249,11 @@
         )
 
     swap = (tile > 0).astype(jnp.int32)
-    edge = (tile == 0) | (tile == nt - 1)
-    swap_edge = (tile == nt - 1).astype(jnp.int32)
+    edge = (tile <= 1) | (tile == nt - 1)
 
     def advance(group, carry):
         lf = jnp.where(edge, lax.rem(group, nf), group // 2)
-        way = jnp.where(edge, lax.rem(group // nf + swap_edge, 2), lax.rem(group + swap, 2))
+        way = jnp.where(edge, lax.rem(group // nf + swap, 2), lax.rem(group + swap, 2))
         opens = jnp.where(edge, group < nf, lax.rem(group, 2) == 0)
         ratio = jnp.float32(ratio_of[0])
         for k in range(1, nf):
@@ -329,19 +301,51 @@
         for i in range(half):
             own[start + i] = xs[i]
 
-        @pl.when(jnp.logical_not(opens) & (lf == 0))
+        @pl.when(group == jnp.where(edge, 0, 1))
         def _():
             pl.semaphore_wait(met, len(greeted))
 
-        @pl.when(jnp.logical_not(opens))
+        @pl.when(edge)
+        def _():
+            for k in order:
+                share_copy(lf, k, way * half, half).start()
+
+        @pl.when(jnp.logical_not(edge | opens))
         def _():
             for k in order:
                 share_copy(lf, k).start()
+
+        @pl.when(jnp.logical_not(opens))
+        def _():
             share_local(lf).start()
 
         return carry
 
     lax.fori_loop(0, 2 * nf, advance, 0)
+
+    small[2].wait()
+    small[3].wait()
+    scaled = small_f[0] * jnp.float32(0.2 * 0.03)
+    small_f[2] = jnp.cos(small_f[1])
+    small_f[3] = jnp.sin(small_f[1])
+    small_f[4] = mask_i.astype(jnp.float32)
+    small_f[5] = scaled
+
+    def mine(k):
+        return jnp.broadcast_to(small_f[k, pl.ds(spec, 1), :], (8, POINTS))
+
+    for target, cos_w, sin_w, scale in (
+        (grow, small_f[2], small_f[3], scaled), (grow_row, mine(2), mine(3), mine(5))
+    ):
+        along, across = scale * cos_w, scale * sin_w
+        for d in range(QUAD):
+            cos_d, sin_d = jnp.float32(math.cos(ANGLE[d])), jnp.float32(math.sin(ANGLE[d]))
+            ahead = along * cos_d + across * sin_d
+            aside = across * cos_d - along * sin_d
+            target[d] = jnp.maximum(ahead, 0.0)
+            target[QUAD + d] = jnp.maximum(aside, 0.0)
+            target[2 * QUAD + d] = jnp.maximum(-ahead, 0.0)
+            target[3 * QUAD + d] = jnp.maximum(-aside, 0.0)
 
     mask_row = mine(4)
     place8 = lax.broadcasted_iota(jnp.int32, (8, POINTS), 0)

time: 26.5 us -> 26.3 us (level)
  no operation moved by 1% of the time
where the time goes in v5:
time: 26.3 us; the launch traced here: 26.2 us
  Pallas kernels  25.4 us (97%)
  local copies, waits for them, and re-layouts  0.76 us (3%)
    pallas_call x1, Pallas kernels, body(): pl.pallas_call(functools.partial(kernel, nt, ns, nf), out_shape=pltpu.VME...  25.4 us
    unnamed x1, local copies, waits for them, and re-layouts  0.76 us

profile of v5, /device:TPU:1, one launch (start us, length us, event | category | flops | bytes accessed | tf_op | source)
XLA Modules:
  0.0 26.2 jit_solution(2736191305945546475)
XLA Ops:
  0.0 25.4 %shard_map.55 = f32[108,8,128]{2,1,0:T(8,128)S(1)} custom-call(f32[108,8,128]{2,1,0:T(8,128)} %spectra.1, f32[8,128]{1,0:T(8,128)} %speed_hbm.1, f32[8,128]{1,0:T(8,128)} %dir_hbm.1, s32[8,128]{1,0:T(8,128)} %mask_hbm.1, s32[4,8]{1,0:T(4,128)} %bitcast.1), custom_call_target="tpu_custom_call" | custom-call | tf_op jit(solution)/shard_map/pallas_call | solution.py:445
  25.4 0.8 %copy.7 = f32[108,8,128]{2,1,0:T(8,128)} copy(f32[108,8,128]{2,1,0:T(8,128)S(1)} %shard_map.55) | data formatting | bytes 884736

commit v6 on v5

--- a/solution.py
+++ b/solution.py
@@ -107,15 +107,21 @@
             device_id={"tile": other}, device_id_type=MESH,
         )
 
+    comes = (tile > 0, tile < nt - 1)
+
+    def start_halos(lf):
+        for way, other, there in ways[::-1]:
+
+            @pl.when(there)
+            def _():
+                halo_copy(lf, way, other).start()
+
     pl.semaphore_wait(
         barrier, len(greeted) + (tile > 0).astype(jnp.int32) + (tile < nt - 1).astype(jnp.int32)
     )
-    comes = (tile > 0, tile < nt - 1)
-    for way, other, there in ways:
-
-        @pl.when(there)
-        def _():
-            halo_copy(0, way, other).start()
+    @pl.when(tile == 0)
+    def _():
+        start_halos(0)
 
     for other in greeted:
         pl.semaphore_signal(met, inc=1, device_id={"spec": other}, device_id_type=MESH)
@@ -147,18 +153,18 @@
         aux_out[way, 1] = jnp.where(west_id >= 0, take_rows(place, west_at), -1)
         aux_out[way, 2] = jnp.where(east_id >= 0, take_rows(place, east_at), -1)
 
-    for way, other, there in ways:
+    for way, other, there in ways[::-1]:
 
         @pl.when(there)
         def _():
             aux_copy(way, other).start()
 
+    @pl.when(tile > 0)
+    def _():
+        start_halos(0)
+
     for lf in range(1, nf):
-        for way, other, there in ways:
-
-            @pl.when(there)
-            def _():
-                halo_copy(lf, way, other).start()
+        start_halos(lf)
 
     for way, other, there in ways:
 

time: 26.3 us -> 26.3 us (level)
  no operation moved by 1% of the time
where the time goes in v6:
time: 26.3 us; the launch traced here: 26.1 us
  Pallas kernels  25.3 us (96%)
  local copies, waits for them, and re-layouts  0.76 us (3%)
    pallas_call x1, Pallas kernels, body(): pl.pallas_call(functools.partial(kernel, nt, ns, nf), out_shape=pltpu.VME...  25.3 us
    unnamed x1, local copies, waits for them, and re-layouts  0.76 us

profile of v6, /device:TPU:1, one launch (start us, length us, event | category | flops | bytes accessed | tf_op | source)
XLA Modules:
  0.0 26.1 jit_solution(10661903085548164054)
XLA Ops:
  0.0 25.3 %shard_map.55 = f32[108,8,128]{2,1,0:T(8,128)S(1)} custom-call(f32[108,8,128]{2,1,0:T(8,128)} %spectra.1, f32[8,128]{1,0:T(8,128)} %speed_hbm.1, f32[8,128]{1,0:T(8,128)} %dir_hbm.1, s32[8,128]{1,0:T(8,128)} %mask_hbm.1, s32[4,8]{1,0:T(4,128)} %bitcast.1), custom_call_target="tpu_custom_call" | custom-call | tf_op jit(solution)/shard_map/pallas_call | solution.py:451
  25.4 0.8 %copy.7 = f32[108,8,128]{2,1,0:T(8,128)} copy(f32[108,8,128]{2,1,0:T(8,128)S(1)} %shard_map.55) | data formatting | bytes 884736

commit v7 on v6

--- a/solution.py
+++ b/solution.py
@@ -218,7 +218,7 @@
             index_t[way, q], index_t[way, 2 + q], index_t[way, 4 + q] = pull, hpull, lanes_of[side]
             factor_t[way, q], factor_t[way, 2 + q] = keep, hkeep
 
-    chunk = NDIR // 6
+    chunk = NDIR // 3
     order = sorted(range(1, ns), key=lambda k: -min(k // 2, (ns - k) // 2))
 
     def peer(k):

time: 26.3 us -> 26.1 us (level)
  no operation moved by 1% of the time
where the time goes in v7:
time: 26.1 us; the launch traced here: 26 us
  Pallas kernels  25.2 us (97%)
  local copies, waits for them, and re-layouts  0.76 us (3%)
    pallas_call x1, Pallas kernels, body(): pl.pallas_call(functools.partial(kernel, nt, ns, nf), out_shape=pltpu.VME...  25.2 us
    unnamed x1, local copies, waits for them, and re-layouts  0.76 us

profile of v7, /device:TPU:1, one launch (start us, length us, event | category | flops | bytes accessed | tf_op | source)
XLA Modules:
  0.0 26.0 jit_solution(9151310836091820828)
XLA Ops:
  0.0 25.2 %shard_map.55 = f32[108,8,128]{2,1,0:T(8,128)S(1)} custom-call(f32[108,8,128]{2,1,0:T(8,128)} %spectra.1, f32[8,128]{1,0:T(8,128)} %speed_hbm.1, f32[8,128]{1,0:T(8,128)} %dir_hbm.1, s32[8,128]{1,0:T(8,128)} %mask_hbm.1, s32[4,8]{1,0:T(4,128)} %bitcast.1), custom_call_target="tpu_custom_call" | custom-call | tf_op jit(solution)/shard_map/pallas_call | solution.py:451
  25.2 0.8 %copy.7 = f32[108,8,128]{2,1,0:T(8,128)} copy(f32[108,8,128]{2,1,0:T(8,128)S(1)} %shard_map.55) | data formatting | bytes 884736
